TPU v7x, 32 devices: a whole 2x2x4 slice. The times are simulated.
32 devices in a mesh: pipe: 2 (over x), dp: 16 (over z, y, core).
Axes of the slice: x: 2, y: 2, z: 4, core: 2. Of those that a mesh axis runs over, the one named last changes fastest.
Arguments:
- inputs: bfloat16 [4, 8192, 768], P(None, 'dp'), may hold values from -6 to 6
- bucket: int32 [4], replicated, may hold values from 128 to 512, as said below
- plan: int32 [4], replicated, may hold values from 0 to 3, each once
- cotangent: bfloat16 [4, 8192, 768], P(None, 'dp'), may hold values from -6 to 6
- norm1_gain: float32 [2, 768], P('pipe'), may hold values from 0.25 to 1.75
- norm1_bias: float32 [2, 768], P('pipe'), may hold values from -2 to 2
- up_weight: bfloat16 [2, 768, 3072], P('pipe'), may hold values from -0.21875 to 0.21875
- up_bias: float32 [2, 3072], P('pipe'), may hold values from -3 to 3
- down_weight: bfloat16 [2, 3072, 768], P('pipe'), may hold values from -0.109375 to 0.109375
- down_bias: float32 [2, 768], P('pipe'), may hold values from -2 to 2
- norm2_gain: float32 [2, 768], P('pipe'), may hold values from 0.25 to 1.75
- norm2_bias: float32 [2, 768], P('pipe'), may hold values from -2 to 2
Outputs:
- activations: float32 [2, 4, 8192, 768], P('pipe', None, 'dp')
- input_grad: float32 [2, 4, 8192, 768], P('pipe', None, 'dp')
- norm1_gain_grad: float32 [2, 768], P('pipe')
- norm1_bias_grad: float32 [2, 768], P('pipe')
- up_weight_grad: float32 [2, 768, 3072], P('pipe')
- up_bias_grad: float32 [2, 3072], P('pipe')
- down_weight_grad: float32 [2, 3072, 768], P('pipe')
- down_bias_grad: float32 [2, 768], P('pipe')
- norm2_gain_grad: float32 [2, 768], P('pipe')
- norm2_bias_grad: float32 [2, 768], P('pipe')
Inputs may be any that keep to these rules, and one draw needn't show every extreme that they name: `bucket`: each entry is 128, 256 or 512; at least one entry is 512. `plan`: a permutation of the slots.
All inputs are finite; a program needn't handle non-finite values.
Results may differ from a plain program's by a relative error of at most 0.01.
Values may be sent and summed in bfloat16 or wider, within the bound.
A program may use at most 256 MiB of HBM per device.

v0:
```python
from functools import partial
import math

import jax
import jax.numpy as jnp
from jax import lax
from jax.sharding import PartitionSpec as P

D = 768
LMAX = 512


def passed_along(block, axis, distance):
    devices = range(lax.axis_size(axis))
    route = [(i - distance, i) for i in devices if i - distance in devices]
    return lax.ppermute(block, axis, route)


def layer_norm(values, gain, offset):
    average = jnp.mean(values, axis=-1, keepdims=True)
    centered = values - average
    variance = jnp.mean(centered * centered, axis=-1, keepdims=True)
    return centered * lax.rsqrt(variance + 1e-06) * gain + offset


def hidden_table():
    positions = jnp.arange(D, dtype=jnp.int32)
    phase = positions[:, None] * positions[None, :] % D
    width_f = jnp.float32(D)
    angle = 2.0 * math.pi * phase.astype(jnp.float32) / width_f
    scale = lax.rsqrt(width_f)
    return jnp.concatenate([jnp.cos(angle) * scale, jnp.sin(angle) * scale], axis=1).astype(
        jnp.bfloat16
    )


def seq_tables(length, width):
    positions = jnp.arange(width, dtype=jnp.int32)
    row_pos = positions[:, None]
    col_pos = positions[None, :]
    same = row_pos // length == col_pos // length
    phase = row_pos % length * (col_pos % length) % length
    length_f = length.astype(jnp.float32)
    angle = 2.0 * math.pi * phase.astype(jnp.float32) / length_f
    scale = lax.rsqrt(length_f)
    cosine = jnp.where(same, jnp.cos(angle) * scale, 0.0).astype(jnp.bfloat16)
    sine = jnp.where(same, jnp.sin(angle) * scale, 0.0).astype(jnp.bfloat16)
    return (cosine, sine)


def apply_table(table, values, width):
    blocks = values.reshape(-1, width, values.shape[-1])
    result = jnp.einsum("ij,bjd->bid", table, blocks, preferred_element_type=jnp.float32)
    return result.reshape(values.shape)


def seq_products(length, left_in, right_in):
    cosine, sine = seq_tables(length, LMAX)
    result = (apply_table(cosine, left_in, LMAX), apply_table(sine, right_in, LMAX))
    return result


def forward_layer(values, length, weights, table):
    gain_one, bias_one, up_matrix, up_offset, down_matrix, down_offset, gain_two, bias_two = weights
    pair_part = jnp.dot(values, table, preferred_element_type=jnp.float32).astype(jnp.bfloat16)
    cos_part, sin_part = seq_products(length, pair_part[:, :D], pair_part[:, D:])
    first_sum = values.astype(jnp.float32) + (cos_part - sin_part)
    normed = layer_norm(first_sum, gain_one, bias_one)
    normed_low = normed.astype(jnp.bfloat16)
    pre_act = jnp.dot(normed_low, up_matrix, preferred_element_type=jnp.float32) + up_offset
    activated = jax.nn.gelu(pre_act, approximate=True).astype(jnp.bfloat16)
    second_sum = normed + (
        jnp.dot(activated, down_matrix, preferred_element_type=jnp.float32) + down_offset
    )
    result = layer_norm(second_sum, gain_two, bias_two)
    return (result, (length, first_sum, normed_low, pre_act, activated, second_sum))


def contract_rows(left_in, right_in):
    return lax.dot_general(
        left_in, right_in, (((0,), (0,)), ((), ())), preferred_element_type=jnp.float32
    )


def contract_cols(left_in, right_in):
    return lax.dot_general(
        left_in, right_in, (((1,), (1,)), ((), ())), preferred_element_type=jnp.float32
    )


def backward_layer(out_grad, stored, weights, table):
    gain_one, bias_one, up_matrix, up_offset, down_matrix, down_offset, gain_two, bias_two = weights
    length, first_sum, normed_low, pre_act, activated, second_sum = stored
    unused, second_back = jax.vjp(layer_norm, second_sum, gain_two, bias_two)
    second_grad, gain_two_grad, bias_two_grad = second_back(out_grad)
    branch_grad = second_grad.astype(jnp.bfloat16)
    down_offset_grad = jnp.sum(branch_grad, axis=0, dtype=jnp.float32)
    down_matrix_grad = contract_rows(activated, branch_grad)
    act_grad = contract_cols(branch_grad, down_matrix)
    unused, gelu_back = jax.vjp(partial(jax.nn.gelu, approximate=True), pre_act)
    pre_grad = gelu_back(act_grad)[0].astype(jnp.bfloat16)
    up_offset_grad = jnp.sum(pre_grad, axis=0, dtype=jnp.float32)
    up_matrix_grad = contract_rows(normed_low, pre_grad)
    normed_grad = second_grad + contract_cols(pre_grad, up_matrix)
    unused, first_back = jax.vjp(layer_norm, first_sum, gain_one, bias_one)
    first_grad, gain_one_grad, bias_one_grad = first_back(normed_grad)
    mix_grad = first_grad.astype(jnp.bfloat16)
    cos_grad, sin_grad = seq_products(length, mix_grad, mix_grad)
    pair_grad = jnp.concatenate(
        [cos_grad.astype(jnp.bfloat16), (-sin_grad).astype(jnp.bfloat16)], axis=1
    )
    in_grad = first_grad + contract_cols(pair_grad, table)
    grads = (
        gain_one_grad,
        bias_one_grad,
        up_matrix_grad,
        up_offset_grad,
        down_matrix_grad,
        down_offset_grad,
        gain_two_grad,
        bias_two_grad,
    )
    return (in_grad, grads)


def per_device(
    inputs,
    bucket,
    plan,
    cotangent,
    norm1_gain,
    norm1_bias,
    up_weight,
    up_bias,
    down_weight,
    down_bias,
    norm2_gain,
    norm2_bias,
):
    section_index = lax.axis_index("pipe")
    is_first = section_index == 0
    weights = tuple(
        (
            p[0]
            for p in (
                norm1_gain,
                norm1_bias,
                up_weight,
                up_bias,
                down_weight,
                down_bias,
                norm2_gain,
                norm2_bias,
            )
        )
    )
    table = hidden_table()
    count = inputs.shape[0]
    stored_list = []
    results = []
    received = jnp.zeros(inputs.shape[1:], jnp.bfloat16)
    for section_tick in range(count + 1):
        own_slot = min(section_tick, count - 1)
        prior_slot = max(section_tick - 1, 0)
        length = jnp.where(is_first, bucket[own_slot], bucket[prior_slot])
        own_input = lax.dynamic_index_in_dim(inputs, plan[own_slot], 0, keepdims=False)
        current = jnp.where(is_first, own_input, received)
        result, kept = forward_layer(current, length, weights, table)
        results.append(result)
        stored_list.append(kept)
        if section_tick < count:
            received = passed_along(result.astype(jnp.bfloat16), "pipe", 1)
    activations = jnp.stack(
        [jnp.where(is_first, results[slot], results[slot + 1]) for slot in range(count)]
    )[None]
    totals = None
    in_grads = []
    arriving = jnp.zeros(inputs.shape[1:], jnp.bfloat16)
    for back_tick in range(count + 1):
        if back_tick < count:
            given = cotangent[count - 1 - back_tick].astype(jnp.float32)
        else:
            given = jnp.zeros(inputs.shape[1:], jnp.float32)
        out_grad = jnp.where(is_first, arriving.astype(jnp.float32), given)
        in_grad, grads = backward_layer(out_grad, stored_list[count - back_tick], weights, table)
        outgoing = in_grad.astype(jnp.bfloat16)
        in_grads.append(jnp.where(is_first, in_grad, outgoing.astype(jnp.float32)))
        totals = grads if totals is None else jax.tree.map(jnp.add, totals, grads)
        if back_tick < count:
            arriving = passed_along(outgoing, "pipe", -1)
    input_grad = jnp.stack(
        [
            jnp.where(is_first, in_grads[count - slot], in_grads[count - 1 - slot])
            for slot in range(count)
        ]
    )[None]
    summed = lax.psum(
        (totals[0], totals[1], totals[2], totals[3], totals[4], totals[5], totals[6], totals[7]),
        "dp",
    )
    return (activations, input_grad) + tuple((piece[None] for piece in summed))


def solution(mesh):
    in_specs = (
        P(None, "dp", None),
        P(),
        P(),
        P(None, "dp", None),
        P("pipe", None),
        P("pipe", None),
        P("pipe", None, None),
        P("pipe", None),
        P("pipe", None, None),
        P("pipe", None),
        P("pipe", None),
        P("pipe", None),
    )
    out_specs = (
        P("pipe", None, "dp", None),
        P("pipe", None, "dp", None),
        P("pipe", None),
        P("pipe", None),
        P("pipe", None, None),
        P("pipe", None),
        P("pipe", None, None),
        P("pipe", None),
        P("pipe", None),
        P("pipe", None),
    )
    return jax.shard_map(
        per_device, mesh=mesh, in_specs=in_specs, out_specs=out_specs, check_vma=False
    )
```

profile of v0, /device:TPU:0, one launch (start us, length us, event | category | flops | bytes accessed | tf_op | source)
XLA Modules:
  0.0 1003.8 jit_solution(3181186315956270941)
XLA Ops:
  17.2 10.8 %multiply_convert_fusion.5 = (bf16[768,768]{1,0:T(8,128)(2,1)}, bf16[768,768]{1,0:T(8,128)(2,1)}) fusion(), kind=kLoop, calls=%fused_computation.118 | loop fusion | flops 7667712 | bytes 2359296 | tf_op jit(solution)/shard_map/convert.4
  38.8 14.5 %fusion.232 = f32[768,512]{1,0:T(8,128)S(1)} fusion(bf16[512,1536]{1,0:T(8,128)(2,1)S(1)} %convolution_convert_fusion.4, f32[]{:T(128)S(6)} %rsqrt.130, s32[512]{0:T(512)S(1)} %get-tuple-element.160, f32[]{:T(128)S(6)} %convert_element_type.431, pred[]{:T(512)S(6)} %lt.171, s32[]{:T(128)S(6)} %select_n.419, s32[512]{0:T(512)S(1)} %get-tuple-element.159), kind=kOutput, calls=%fused_computation.357 | convolution fusion | flops 406585344 | bytes 2367501 | tf_op jit(solution)/shard_map/ij,bjd->bid/dot_general | solution.py:53
  53.3 14.3 %fusion.400 = (f32[512]{0:T(512)S(1)}, f32[512,768]{0,1:T(8,128)S(1)}, f32[768,512]{1,0:T(8,128)S(1)}) fusion(bf16[1,512,768]{1,2,0:T(8,128)(2,1)S(1)} %copy.62, pred[]{:T(512)S(6)} %eq.77, f32[768,512]{1,0:T(8,128)S(1)} %fusion.232, f32[]{:T(128)S(6)} %rsqrt.130, s32[512]{0:T(512)S(1)} %get-tuple-element.160, f32[]{:T(128)S(6)} %convert_element_type.431, ...), kind=kOutput, calls=%fused_computation.571 | convolution fusion | flops 408550912 | bytes 6301710 | tf_op jit(solution)/shard_map/ij,bjd->bid/dot_general | solution.py:53
  83.9 14.4 %collective-permute-done = bf16[512,768]{0,1:T(8,128)(2,1)} collective-permute-done((bf16[512,768]{0,1:T(8,128)(2,1)}, bf16[512,768]{0,1:T(8,128)(2,1)}, u32[]{:S(2)}, u32[]{:S(2)}) %collective-permute-start) | collective-permute-done | bytes 786464 | tf_op jit(solution)/shard_map/ppermute | solution.py:16
  101.4 14.2 %fusion.229 = f32[768,512]{1,0:T(8,128)S(1)} fusion(bf16[512,1536]{1,0:T(8,128)(2,1)S(1)} %convolution_convert_fusion.3, f32[]{:T(128)S(6)} %rsqrt.133, s32[512]{0:T(512)S(1)} %get-tuple-element.162, f32[]{:T(128)S(6)} %convert_element_type.442, pred[]{:T(512)S(6)} %lt.175, s32[]{:T(128)S(6)} %select_n.428, s32[512]{0:T(512)S(1)} %get-tuple-element.161), kind=kOutput, calls=%fused_computation.354 | convolution fusion | flops 406585344 | bytes 2367501 | tf_op jit(solution)/shard_map/ij,bjd->bid/dot_general | solution.py:53
  115.6 14.6 %fusion.406 = (f32[512]{0:T(512)S(1)}, f32[512,768]{0,1:T(8,128)S(1)}) fusion(f32[768,512]{1,0:T(8,128)S(1)} %fusion.229, f32[]{:T(128)S(6)} %rsqrt.133, s32[512]{0:T(512)S(1)} %get-tuple-element.162, f32[]{:T(128)S(6)} %convert_element_type.442, pred[]{:T(512)S(6)} %lt.175, s32[]{:T(128)S(6)} %select_n.428, s32[512]{0:T(512)S(1)} %get-tuple-element.161, ...), kind=kOutput, calls=%fused_computation.577 | convolution fusion | flops 408550912 | bytes 5515278 | tf_op jit(solution)/shard_map/ij,bjd->bid/dot_general | solution.py:53
  149.3 11.6 %collective-permute-done.1 = bf16[512,768]{0,1:T(8,128)(2,1)} collective-permute-done((bf16[512,768]{0,1:T(8,128)(2,1)}, bf16[512,768]{0,1:T(8,128)(2,1)}, u32[]{:S(2)}, u32[]{:S(2)}) %collective-permute-start.1) | collective-permute-done | bytes 786464 | tf_op jit(solution)/shard_map/ppermute | solution.py:16
  164.3 14.4 %fusion.226 = f32[768,512]{1,0:T(8,128)S(1)} fusion(bf16[512,1536]{1,0:T(8,128)(2,1)S(1)} %convolution_convert_fusion.2, f32[]{:T(128)S(6)} %rsqrt.136, s32[512]{0:T(512)S(1)} %get-tuple-element.164, f32[]{:T(128)S(6)} %convert_element_type.451, pred[]{:T(512)S(6)} %lt.179, s32[]{:T(128)S(6)} %select_n.438, s32[512]{0:T(512)S(1)} %get-tuple-element.163), kind=kOutput, calls=%fused_computation.351 | convolution fusion | flops 406585344 | bytes 2367501 | tf_op jit(solution)/shard_map/ij,bjd->bid/dot_general | solution.py:53
  178.8 14.4 %fusion.408 = (f32[512]{0:T(512)S(1)}, f32[512,768]{0,1:T(8,128)S(1)}) fusion(f32[768,512]{1,0:T(8,128)S(1)} %fusion.226, f32[]{:T(128)S(6)} %rsqrt.136, s32[512]{0:T(512)S(1)} %get-tuple-element.164, f32[]{:T(128)S(6)} %convert_element_type.451, pred[]{:T(512)S(6)} %lt.179, s32[]{:T(128)S(6)} %select_n.438, s32[512]{0:T(512)S(1)} %get-tuple-element.163, ...), kind=kOutput, calls=%fused_computation.579 | convolution fusion | flops 408550912 | bytes 5515278 | tf_op jit(solution)/shard_map/ij,bjd->bid/dot_general | solution.py:53
  213.3 12.4 %collective-permute-done.2 = bf16[512,768]{0,1:T(8,128)(2,1)S(1)} collective-permute-done((bf16[512,768]{0,1:T(8,128)(2,1)}, bf16[512,768]{0,1:T(8,128)(2,1)S(1)}, u32[]{:S(2)}, u32[]{:S(2)}) %collective-permute-start.2) | collective-permute-done | bytes 786464 | tf_op jit(solution)/shard_map/ppermute | solution.py:16
  228.4 14.2 %fusion.223 = f32[768,512]{1,0:T(8,128)S(1)} fusion(bf16[512,1536]{1,0:T(8,128)(2,1)S(1)} %convolution_convert_fusion.1, f32[]{:T(128)S(6)} %rsqrt.139, s32[512]{0:T(512)S(1)} %get-tuple-element.166, f32[]{:T(128)S(6)} %convert_element_type.460, pred[]{:T(512)S(6)} %lt.183, s32[]{:T(128)S(6)} %select_n.448, s32[512]{0:T(512)S(1)} %get-tuple-element.165), kind=kOutput, calls=%fused_computation.348 | convolution fusion | flops 406585344 | bytes 2367501 | tf_op jit(solution)/shard_map/ij,bjd->bid/dot_general | solution.py:53
  242.6 14.6 %fusion.410 = (f32[512]{0:T(512)S(1)}, f32[512,768]{0,1:T(8,128)S(1)}) fusion(f32[768,512]{1,0:T(8,128)S(1)} %fusion.223, f32[]{:T(128)S(6)} %rsqrt.139, s32[512]{0:T(512)S(1)} %get-tuple-element.166, f32[]{:T(128)S(6)} %convert_element_type.460, pred[]{:T(512)S(6)} %lt.183, s32[]{:T(128)S(6)} %select_n.448, s32[512]{0:T(512)S(1)} %get-tuple-element.165, ...), kind=kOutput, calls=%fused_computation.581 | convolution fusion | flops 408550912 | bytes 5515278 | tf_op jit(solution)/shard_map/ij,bjd->bid/dot_general | solution.py:53
  287.7 14.4 %fusion.220 = f32[768,512]{1,0:T(8,128)S(1)} fusion(bf16[512,1536]{1,0:T(8,128)(2,1)S(1)} %convolution_convert_fusion, f32[]{:T(128)S(6)} %rsqrt.142, s32[512]{0:T(512)S(1)} %add_select_fusion.7, f32[]{:T(128)S(6)} %convert_element_type.469, pred[]{:T(512)S(6)} %lt.186, s32[]{:T(128)S(6)} %select_n.456, s32[512]{0:T(512)S(1)} %add_select_fusion.6), kind=kOutput, calls=%fused_computation.345 | convolution fusion | flops 406585344 | bytes 2367501 | tf_op jit(solution)/shard_map/ij,bjd->bid/dot_general | solution.py:53
  302.2 14.3 %fusion.412 = (f32[512]{0:T(512)S(1)}, f32[512,768]{0,1:T(8,128)S(1)}) fusion(f32[768,512]{1,0:T(8,128)S(1)} %fusion.220, f32[]{:T(128)S(6)} %rsqrt.142, s32[512]{0:T(512)S(1)} %add_select_fusion.7, f32[]{:T(128)S(6)} %convert_element_type.469, pred[]{:T(512)S(6)} %lt.186, s32[]{:T(128)S(6)} %select_n.456, s32[512]{0:T(512)S(1)} %add_select_fusion.6, ...), kind=kOutput, calls=%fused_computation.583 | convolution fusion | flops 408550912 | bytes 5515278 | tf_op jit(solution)/shard_map/ij,bjd->bid/dot_general | solution.py:53
  344.0 15.1 %fusion.154 = bf16[512,768]{0,1:T(8,128)(2,1)S(1)} fusion(f32[]{:T(128)S(6)} %rsqrt.142, s32[512]{0:T(512)S(1)} %add_select_fusion.7, f32[]{:T(128)S(6)} %convert_element_type.469, pred[]{:T(512)S(6)} %lt.186, s32[]{:T(128)S(6)} %select_n.456, s32[512]{0:T(512)S(1)} %add_select_fusion.6, f32[512,768]{0,1:T(8,128)S(1)} %get-tuple-element.85, ...), kind=kOutput, calls=%fused_computation.276 | convolution fusion | flops 408158208 | bytes 2365453 | tf_op jit(solution)/shard_map/ij,bjd->bid/dot_general | solution.py:53
  359.2 14.9 %fusion.149 = bf16[512,768]{0,1:T(8,128)(2,1)S(1)} fusion(f32[]{:T(128)S(6)} %rsqrt.142, s32[512]{0:T(512)S(1)} %add_select_fusion.7, f32[]{:T(128)S(6)} %convert_element_type.469, pred[]{:T(512)S(6)} %lt.186, s32[]{:T(128)S(6)} %select_n.456, s32[512]{0:T(512)S(1)} %add_select_fusion.6, f32[512,768]{0,1:T(8,128)S(1)} %get-tuple-element.85, ...), kind=kOutput, calls=%fused_computation.271 | convolution fusion | flops 407764992 | bytes 2365453 | tf_op jit(solution)/shard_map/ij,bjd->bid/dot_general | solution.py:53
  389.2 10.8 %collective-permute-done.4 = bf16[512,768]{0,1:T(8,128)(2,1)S(1)} collective-permute-done((bf16[512,768]{0,1:T(8,128)(2,1)S(1)}, bf16[512,768]{0,1:T(8,128)(2,1)S(1)}, u32[]{:S(2)}, u32[]{:S(2)}) %collective-permute-start.4) | collective-permute-done | bytes 786464 | tf_op jit(solution)/shard_map/ppermute | solution.py:16
  402.8 8.6 convert_reduce_fusion.3
  415.7 15.1 %fusion.155 = bf16[512,768]{0,1:T(8,128)(2,1)S(1)} fusion(f32[]{:T(128)S(6)} %rsqrt.139, s32[512]{0:T(512)S(1)} %get-tuple-element.166, f32[]{:T(128)S(6)} %convert_element_type.460, pred[]{:T(512)S(6)} %lt.183, s32[]{:T(128)S(6)} %select_n.448, s32[512]{0:T(512)S(1)} %get-tuple-element.165, f32[512,768]{0,1:T(8,128)S(1)} %get-tuple-element.81, ...), kind=kOutput, calls=%fused_computation.277 | convolution fusion | flops 408158208 | bytes 2365453 | tf_op jit(solution)/shard_map/ij,bjd->bid/dot_general | solution.py:53
  430.8 14.9 %fusion.150 = bf16[512,768]{0,1:T(8,128)(2,1)S(1)} fusion(f32[]{:T(128)S(6)} %rsqrt.139, s32[512]{0:T(512)S(1)} %get-tuple-element.166, f32[]{:T(128)S(6)} %convert_element_type.460, pred[]{:T(512)S(6)} %lt.183, s32[]{:T(128)S(6)} %select_n.448, s32[512]{0:T(512)S(1)} %get-tuple-element.165, f32[512,768]{0,1:T(8,128)S(1)} %get-tuple-element.81, ...), kind=kOutput, calls=%fused_computation.272 | convolution fusion | flops 407764992 | bytes 2365453 | tf_op jit(solution)/shard_map/ij,bjd->bid/dot_general | solution.py:53
  472.3 8.7 convert_reduce_fusion.2
  484.9 15.1 %fusion.156 = bf16[512,768]{0,1:T(8,128)(2,1)S(1)} fusion(f32[]{:T(128)S(6)} %rsqrt.136, s32[512]{0:T(512)S(1)} %copy-done.107, f32[]{:T(128)S(6)} %convert_element_type.451, pred[]{:T(512)S(6)} %lt.179, s32[]{:T(128)S(6)} %select_n.438, s32[512]{0:T(512)S(1)} %copy-done.105, f32[512,768]{0,1:T(8,128)S(1)} %get-tuple-element.77, ...), kind=kOutput, calls=%fused_computation.278 | convolution fusion | flops 408158208 | bytes 2365453 | tf_op jit(solution)/shard_map/ij,bjd->bid/dot_general | solution.py:53
  500.1 14.9 %fusion.151 = bf16[512,768]{0,1:T(8,128)(2,1)S(1)} fusion(f32[]{:T(128)S(6)} %rsqrt.136, s32[512]{0:T(512)S(1)} %copy-done.107, f32[]{:T(128)S(6)} %convert_element_type.451, pred[]{:T(512)S(6)} %lt.179, s32[]{:T(128)S(6)} %select_n.438, s32[512]{0:T(512)S(1)} %copy-done.105, f32[512,768]{0,1:T(8,128)S(1)} %get-tuple-element.77, ...), kind=kOutput, calls=%fused_computation.273 | convolution fusion | flops 407764992 | bytes 2365453 | tf_op jit(solution)/shard_map/ij,bjd->bid/dot_general | solution.py:53
  551.5 15.1 %fusion.157 = bf16[512,768]{0,1:T(8,128)(2,1)S(1)} fusion(f32[]{:T(128)S(6)} %rsqrt.133, s32[512]{0:T(512)S(1)} %copy-done.103, f32[]{:T(128)S(6)} %convert_element_type.442, pred[]{:T(512)S(6)} %lt.175, s32[]{:T(128)S(6)} %select_n.428, s32[512]{0:T(512)S(1)} %copy-done.101, f32[512,768]{0,1:T(8,128)S(1)} %get-tuple-element.73, ...), kind=kOutput, calls=%fused_computation.279 | convolution fusion | flops 408158208 | bytes 2365453 | tf_op jit(solution)/shard_map/ij,bjd->bid/dot_general | solution.py:53
  566.7 14.9 %fusion.152 = bf16[512,768]{0,1:T(8,128)(2,1)S(1)} fusion(f32[]{:T(128)S(6)} %rsqrt.133, s32[512]{0:T(512)S(1)} %copy-done.103, f32[]{:T(128)S(6)} %convert_element_type.442, pred[]{:T(512)S(6)} %lt.175, s32[]{:T(128)S(6)} %select_n.428, s32[512]{0:T(512)S(1)} %copy-done.101, f32[512,768]{0,1:T(8,128)S(1)} %get-tuple-element.73, ...), kind=kOutput, calls=%fused_computation.274 | convolution fusion | flops 407764992 | bytes 2365453 | tf_op jit(solution)/shard_map/ij,bjd->bid/dot_general | solution.py:53
  617.3 18.9 %add_bitcast_fusion = f32[1,3072,768]{2,1,0:T(8,128)} fusion(f32[3072,768]{1,0:T(8,128)} %fusion.388, f32[3072,768]{1,0:T(8,128)} %fusion.389, f32[3072,768]{1,0:T(8,128)} %fusion.391, f32[3072,768]{1,0:T(8,128)} %fusion.390, bf16[512,768]{0,1:T(8,128)(2,1)} %copy-done.28, f32[512,3072]{1,0:T(8,128)} %copy-done.6, f32[3072]{0:T(1024)S(1)} %bitcast.358), kind=kOutput, calls=%fused_computation | convolution fusion | flops 2441084928 | bytes 54276096 | tf_op jit(solution)/shard_map/dot_general | solution.py:80
  636.3 16.8 %add_bitcast_fusion.1 = f32[1,768,3072]{2,1,0:T(8,128)} fusion(f32[768,3072]{1,0:T(8,128)} %fusion.383, f32[768,3072]{1,0:T(8,128)} %fusion.380, f32[768,3072]{1,0:T(8,128)} %fusion.374, f32[768,3072]{1,0:T(8,128)} %fusion.377, bf16[512,3072]{1,0:T(8,128)(2,1)} %get-tuple-element.148, f32[512,768]{0,1:T(8,128)S(1)} %copy-done.16, f32[768]{0:T(1024)S(1)} %reduce.2, ...), kind=kOutput, calls=%fused_computation.1 | convolution fusion | flops 2427322368 | bytes 51914752 | tf_op jit(solution)/shard_map/dot_general | solution.py:80
  674.9 14.7 %fusion.153 = bf16[512,768]{0,1:T(8,128)(2,1)S(1)} fusion(f32[]{:T(128)S(6)} %rsqrt.130, s32[512]{0:T(512)S(1)} %copy-done.99, f32[]{:T(128)S(6)} %convert_element_type.431, pred[]{:T(512)S(6)} %lt.171, s32[]{:T(128)S(6)} %select_n.419, s32[512]{0:T(512)S(1)} %copy-done.97, f32[512,768]{0,1:T(8,128)S(1)} %get-tuple-element.71, f32[512]{0:T(512)S(1)} %negate_multiply_fusion), kind=kOutput, calls=%fused_computation.275 | convolution fusion | flops 407764992 | bytes 2365453 | tf_op jit(solution)/shard_map/ij,bjd->bid/dot_general | solution.py:53
  689.6 14.9 %fusion.158 = bf16[512,768]{0,1:T(8,128)(2,1)S(1)} fusion(f32[]{:T(128)S(6)} %rsqrt.130, s32[512]{0:T(512)S(1)} %copy-done.99, f32[]{:T(128)S(6)} %convert_element_type.431, pred[]{:T(512)S(6)} %lt.171, s32[]{:T(128)S(6)} %select_n.419, s32[512]{0:T(512)S(1)} %copy-done.97, f32[512,768]{0,1:T(8,128)S(1)} %get-tuple-element.71, f32[512]{0:T(512)S(1)} %negate_multiply_fusion), kind=kOutput, calls=%fused_computation.280 | convolution fusion | flops 408158208 | bytes 2365453 | tf_op jit(solution)/shard_map/ij,bjd->bid/dot_general | solution.py:53
  716.7 61.8 %all-reduce = (f32[1,768]{1,0:T(1,128)}, f32[1,768]{1,0:T(1,128)}, f32[1,3072]{1,0:T(1,128)}, f32[1,768]{1,0:T(1,128)}, f32[1,768]{1,0:T(1,128)}, /*index=5*/f32[1,768]{1,0:T(1,128)}) all-reduce(f32[1,768]{1,0:T(1,128)S(1)} %broadcast_in_dim.199, f32[1,768]{1,0:T(1,128)S(1)} %broadcast_in_dim.200, ...), channel_id=1, replica_groups=mesh['pipe'=2,'dp'=16] {'dp'}, use_global_device_ids=true, to_apply=%region_45.46 | all-reduce | flops 6912 | bytes 55296 | tf_op jit(solution)/shard_map/psum | solution.py:197
  778.5 205.8 %all-reduce.4.cloned.1.call-done = (f32[1,768,3072]{2,1,0:T(8,128)}, f32[1,3072,768]{2,1,0:T(8,128)}) async-done(((f32[1,768,3072]{2,1,0:T(8,128)}, f32[1,3072,768]{2,1,0:T(8,128)}), (f32[1,768,3072]{2,1,0:T(8,128)}, f32[1,3072,768]{2,1,0:T(8,128)})) %all-reduce.4.cloned.1.call-update) | async-done | bytes 18874384 | tf_op jit(solution)/shard_map/psum | solution.py:197
  984.3 8.8 copy.69
  (449 shorter events, 287.5 us)
Async XLA Ops:
  7.2 21.6 %copy-start.94 = (f32[1,768]{1,0:T(1,128)S(1)}, f32[1,768]{1,0:T(1,128)}, u32[]{:S(2)}) copy-start(f32[1,768]{1,0:T(1,128)} %param.21) | copy-start | bytes 9220
  7.2 21.6 %copy-start.95 = (f32[1,768]{1,0:T(1,128)S(1)}, f32[1,768]{1,0:T(1,128)}, u32[]{:S(2)}) copy-start(f32[1,768]{1,0:T(1,128)} %param.23) | copy-start | bytes 9220
  7.2 977.0 %all-reduce.4.cloned.1.call-start = ((), (), s32[]{:S(2)}) async-start(), calls=%async_computation | async-start | bytes 37748736 | tf_op jit(solution)/shard_map/psum | solution.py:197
  38.7 29.2 %slice-start = ((s8[4718592]{0:T(1024)(128)(4,1)}), s8[4194304]{0:T(1024)(128)(4,1)S(1)}, s32[]{:S(2)}) async-start(s8[4718592]{0:T(1024)(128)(4,1)} %bitcast.325), calls=%async_computation.1 | async-start | bytes 8388608
  74.9 126.6 %copy-start = (f32[512,768]{0,1:T(8,128)}, f32[512,768]{0,1:T(8,128)S(1)}, u32[]{:S(2)}) copy-start(f32[512,768]{0,1:T(8,128)S(1)} %get-tuple-element.119) | copy-start | bytes 4718596
  74.9 126.6 %copy-start.43 = (f32[512]{0:T(512)}, f32[512]{0:T(512)S(1)}, u32[]{:S(2)}) copy-start(f32[512]{0:T(512)S(1)} %broadcast_multiply_fusion.8) | copy-start | bytes 6148
  75.2 126.4 %copy-start.57 = (f32[512]{0:T(512)}, f32[512]{0:T(512)S(1)}, u32[]{:S(2)}) copy-start(f32[512]{0:T(512)S(1)} %fusion.298) | copy-start | bytes 6148
  76.4 21.9 %collective-permute-start = (bf16[512,768]{0,1:T(8,128)(2,1)}, bf16[512,768]{0,1:T(8,128)(2,1)}, u32[]{:S(2)}, u32[]{:S(2)}) collective-permute-start(bf16[512,768]{0,1:T(8,128)(2,1)} %fusion.160), channel_id=1, source_target_pairs={{0,16},{1,17},{2,18},{3,19},{4,20},{5,21},{6,22},{7,23},{8,24},{9,... | collective-permute-start | bytes 2359304 | tf_op jit(solution)/shard_map/ppermute | solution.py:16
  83.9 31.7 %copy-start.100 = (s32[512]{0:T(512)}, s32[512]{0:T(512)S(1)}, u32[]{:S(2)}) copy-start(s32[512]{0:T(512)S(1)} %get-tuple-element.161) | copy-start | bytes 6148
  83.9 31.7 %copy-start.102 = (s32[512]{0:T(512)}, s32[512]{0:T(512)S(1)}, u32[]{:S(2)}) copy-start(s32[512]{0:T(512)S(1)} %get-tuple-element.162) | copy-start | bytes 6148
  101.4 29.2 %slice-start.2 = ((s8[4718592]{0:T(1024)(128)(4,1)}), s8[4194304]{0:T(1024)(128)(4,1)S(1)}, s32[]{:S(2)}) async-start(s8[4718592]{0:T(1024)(128)(4,1)} %bitcast.327), calls=%async_computation.3 | async-start | bytes 8388608
  137.4 64.1 %copy-start.2 = (f32[512,768]{0,1:T(8,128)}, f32[512,768]{0,1:T(8,128)S(1)}, u32[]{:S(2)}) copy-start(f32[512,768]{0,1:T(8,128)S(1)} %get-tuple-element.123) | copy-start | bytes 4718596
  137.4 64.1 %copy-start.47 = (f32[512]{0:T(512)}, f32[512]{0:T(512)S(1)}, u32[]{:S(2)}) copy-start(f32[512]{0:T(512)S(1)} %broadcast_multiply_fusion.6) | copy-start | bytes 6148
  137.7 63.9 %copy-start.55 = (f32[512]{0:T(512)}, f32[512]{0:T(512)S(1)}, u32[]{:S(2)}) copy-start(f32[512]{0:T(512)S(1)} %fusion.300) | copy-start | bytes 6148
  138.9 22.0 %collective-permute-start.1 = (bf16[512,768]{0,1:T(8,128)(2,1)}, bf16[512,768]{0,1:T(8,128)(2,1)}, u32[]{:S(2)}, u32[]{:S(2)}) collective-permute-start(bf16[512,768]{0,1:T(8,128)(2,1)} %fusion.213), channel_id=1, source_target_pairs={{0,16},{1,17},{2,18},{3,19},{4,20},{5,21},{6,22},{7,23},{8,24},{9,... | collective-permute-start | bytes 2359304 | tf_op jit(solution)/shard_map/ppermute | solution.py:16
  149.3 29.4 %copy-start.104 = (s32[512]{0:T(512)}, s32[512]{0:T(512)S(1)}, u32[]{:S(2)}) copy-start(s32[512]{0:T(512)S(1)} %get-tuple-element.163) | copy-start | bytes 6148
  149.3 29.4 %copy-start.106 = (s32[512]{0:T(512)}, s32[512]{0:T(512)S(1)}, u32[]{:S(2)}) copy-start(s32[512]{0:T(512)S(1)} %get-tuple-element.164) | copy-start | bytes 6148
  164.2 29.9 %slice-start.4 = ((s8[4718592]{0:T(1024)(128)(4,1)}), s8[4194304]{0:T(1024)(128)(4,1)S(1)}, s32[]{:S(2)}) async-start(s8[4718592]{0:T(1024)(128)(4,1)} %bitcast.329), calls=%async_computation.5 | async-start | bytes 8388608
  204.3 21.3 %collective-permute-start.2 = (bf16[512,768]{0,1:T(8,128)(2,1)}, bf16[512,768]{0,1:T(8,128)(2,1)S(1)}, u32[]{:S(2)}, u32[]{:S(2)}) collective-permute-start(bf16[512,768]{0,1:T(8,128)(2,1)} %get-tuple-element.98), channel_id=1, source_target_pairs={{0,16},{1,17},{2,18},{3,19},{4,20},{5,21},{6,22},{7,23},{8,24},{9,... | collective-permute-start | bytes 2359304 | tf_op jit(solution)/shard_map/ppermute | solution.py:16
  213.1 29.5 %copy-start.40 = (bf16[1,512,768]{1,2,0:T(8,128)(2,1)}, bf16[1,512,768]{1,2,0:T(8,128)(2,1)S(1)}, u32[]{:S(2)}) copy-start(bf16[1,512,768]{1,2,0:T(8,128)(2,1)S(1)} %copy.28) | copy-start | bytes 2359300
  228.4 29.1 %slice-start.6 = ((s8[4718592]{0:T(1024)(128)(4,1)}), s8[4194304]{0:T(1024)(128)(4,1)S(1)}, s32[]{:S(2)}) async-start(s8[4718592]{0:T(1024)(128)(4,1)} %bitcast.331), calls=%async_computation.7 | async-start | bytes 8388608
  265.7 18.6 %collective-permute-start.3 = (bf16[512,768]{0,1:T(8,128)(2,1)}, bf16[512,768]{0,1:T(8,128)(2,1)}, u32[]{:S(2)}, u32[]{:S(2)}) collective-permute-start(bf16[512,768]{0,1:T(8,128)(2,1)} %fusion.215), channel_id=1, source_target_pairs={{0,16},{1,17},{2,18},{3,19},{4,20},{5,21},{6,22},{7,23},{8,24},{9,... | collective-permute-start | bytes 2359304 | tf_op jit(solution)/shard_map/ppermute | solution.py:16
  278.2 61.4 %copy-start.7 = (bf16[1,512,768]{1,2,0:T(8,128)(2,1)}, bf16[1,512,768]{1,2,0:T(8,128)(2,1)S(1)}, u32[]{:S(2)}) copy-start(bf16[1,512,768]{1,2,0:T(8,128)(2,1)S(1)} %copy.63) | copy-start | bytes 2359300
  287.7 29.1 %slice-start.8 = ((s8[4718592]{0:T(1024)(128)(4,1)}), s8[4194304]{0:T(1024)(128)(4,1)S(1)}, s32[]{:S(2)}) async-start(s8[4718592]{0:T(1024)(128)(4,1)} %bitcast.333), calls=%async_computation.9 | async-start | bytes 8388608
  379.3 23.6 %slice-start.16 = ((s8[6291456]{0:T(1024)(128)(4,1)}), s8[4194304]{0:T(1024)(128)(4,1)S(1)}, s32[]{:S(2)}) async-start(s8[6291456]{0:T(1024)(128)(4,1)} %bitcast.341), calls=%async_computation.17 | async-start | bytes 8388608
  380.7 22.2 %slice-start.17 = ((s8[6291456]{0:T(1024)(128)(4,1)}), s8[2097152]{0:T(1024)(128)(4,1)S(1)}, s32[]{:S(2)}) async-start(s8[6291456]{0:T(1024)(128)(4,1)} %bitcast.341), calls=%async_computation.18 | async-start | bytes 4194304
  380.7 19.3 %collective-permute-start.4 = (bf16[512,768]{0,1:T(8,128)(2,1)S(1)}, bf16[512,768]{0,1:T(8,128)(2,1)S(1)}, u32[]{:S(2)}, u32[]{:S(2)}) collective-permute-start(bf16[512,768]{0,1:T(8,128)(2,1)S(1)} %get-tuple-element.137), channel_id=1, source_target_pairs={{16,0},{17,1},{18,2},{19,3},{20,4},{21,5},{22,6},{23,7},{24,8},{25... | collective-permute-start | bytes 2359304 | tf_op jit(solution)/shard_map/ppermute | solution.py:16
  452.5 17.0 %collective-permute-start.5 = (bf16[512,768]{0,1:T(8,128)(2,1)S(1)}, bf16[512,768]{0,1:T(8,128)(2,1)S(1)}, u32[]{:S(2)}, u32[]{:S(2)}) collective-permute-start(bf16[512,768]{0,1:T(8,128)(2,1)S(1)} %get-tuple-element.140), channel_id=1, source_target_pairs={{16,0},{17,1},{18,2},{19,3},{20,4},{21,5},{22,6},{23,7},{24,8},{25... | collective-permute-start | bytes 2359304 | tf_op jit(solution)/shard_map/ppermute | solution.py:16
  521.6 16.2 %collective-permute-start.6 = (bf16[512,768]{0,1:T(8,128)(2,1)S(1)}, bf16[512,768]{0,1:T(8,128)(2,1)S(1)}, u32[]{:S(2)}, u32[]{:S(2)}) collective-permute-start(bf16[512,768]{0,1:T(8,128)(2,1)S(1)} %get-tuple-element.143), channel_id=1, source_target_pairs={{16,0},{17,1},{18,2},{19,3},{20,4},{21,5},{22,6},{23,7},{24,8},{25... | collective-permute-start | bytes 2359304 | tf_op jit(solution)/shard_map/ppermute | solution.py:16
  588.2 21.6 %slice-start.10 = ((s8[6291456]{0:T(1024)(128)(4,1)}), s8[2097152]{0:T(1024)(128)(4,1)S(1)}, s32[]{:S(2)}) async-start(s8[6291456]{0:T(1024)(128)(4,1)} %bitcast.335), calls=%async_computation.11 | async-start | bytes 4194304
  588.2 21.6 %slice-start.26 = ((s8[4718592]{0:T(1024)(128)(4,1)}), s8[4194304]{0:T(1024)(128)(4,1)S(1)}, s32[]{:S(2)}) async-start(s8[4718592]{0:T(1024)(128)(4,1)} %bitcast.367), calls=%async_computation.27 | async-start | bytes 8388608
  591.3 15.3 %collective-permute-start.7 = (bf16[512,768]{0,1:T(8,128)(2,1)S(1)}, bf16[512,768]{0,1:T(8,128)(2,1)S(1)}, u32[]{:S(2)}, u32[]{:S(2)}) collective-permute-start(bf16[512,768]{0,1:T(8,128)(2,1)S(1)} %get-tuple-element.103), channel_id=1, source_target_pairs={{16,0},{17,1},{18,2},{19,3},{20,4},{21,5},{22,6},{23,7},{24,8},{25... | collective-permute-start | bytes 2359304 | tf_op jit(solution)/shard_map/ppermute | solution.py:16
  (113 other events, 976.5 us)
Sparse Core Ops, SparseCore 0:
  653.2 330.9 all-reduce.3
where the time goes:
time: 1010 us; the launch traced here: 1000 us
  matrix products  499 us (49%)
  waiting for transfers between devices  279 us (28%)
  blocking collectives  61.8 us (6%)
  local copies, waits for them, and re-layouts  51 us (5%)
  other arithmetic  49.3 us (5%)
  between operations  33.5 us (3%)
  starting transfers between devices  29.8 us (3%)
    dot_general x20, matrix products, apply_table(): jnp.einsum('ij,bjd->bid', table, blocks, preferred_element_type=jnp.float32)  294 us
    psum x1, waiting for transfers between devices, per_device(): lax.psum((totals[0], totals[1], totals[2], totals[3], totals[4], totals[5...  206 us
    dot_general x10, matrix products, contract_rows(): lax.dot_general(left_in, right_in, (((0,), (0,)), ((), ())), preferred_el...  84.9 us
    ppermute x8, waiting for transfers between devices, passed_along(): return lax.ppermute(block, axis, route)  73.3 us
    dot_general x15, matrix products, contract_cols(): lax.dot_general(left_in, right_in, (((1,), (1,)), ((), ())), preferred_el...  69.4 us
    psum x1, blocking collectives, per_device(): lax.psum((totals[0], totals[1], totals[2], totals[3], totals[4], totals[5...  61.8 us
    unnamed x281, local copies, waits for them, and re-layouts  37.8 us
    ppermute x8, starting transfers between devices, passed_along(): return lax.ppermute(block, axis, route)  29.8 us
  transfers between devices with their start and end apart: 9, of which 9 were waited for; matrix products, arithmetic and copies ran while one was open for 10% of the time, Pallas kernels for 0%

commit v1 on v0

v1 whole, which is shorter than its diff:
```python
import functools
import math

import jax
import jax.numpy as jnp
import ml_dtypes
import numpy as np
from jax import lax
from jax.experimental import pallas as pl
from jax.experimental.pallas import tpu as pltpu
from jax.sharding import PartitionSpec as P

BF = jnp.bfloat16
F32 = jnp.float32
TANH_IN = math.sqrt(2.0 / math.pi)
TANH_CUBE = TANH_IN * 0.044715
EPS = 1e-6
CHUNKS = 4


def hidden_tables(width):
    position = np.arange(width)
    angle = 2.0 * np.pi * (np.outer(position, position) % width) / width
    pair = np.stack([np.cos(angle), np.sin(angle)]) / np.sqrt(width)
    return pair.astype(ml_dtypes.bfloat16)


def seq_tables(rows):
    position = np.arange(rows)
    found = []
    for length in (rows // 4, rows // 2, rows):
        same = position[:, None] // length == position[None, :] // length
        phase = (position[:, None] % length) * (position[None, :] % length) % length
        angle = 2.0 * np.pi * phase / length
        found.append(
            np.stack(
                [
                    np.where(same, np.cos(angle), 0.0) / np.sqrt(length),
                    np.where(same, -np.sin(angle), 0.0) / np.sqrt(length),
                ]
            )
        )
    return np.stack(found).astype(ml_dtypes.bfloat16)


def dot(left, right):
    return jnp.dot(left, right, preferred_element_type=F32)


def dot_t(left, right):
    return lax.dot_general(left, right, (((1,), (1,)), ((), ())), preferred_element_type=F32)


def fold8(values):
    return jnp.sum(values.reshape(-1, 8, values.shape[-1]), axis=0)


def layers_kernel(
    count, rows, width, blocks, fb,
    bucket, plan, norm_ref, upb_ref, in_hbm, cot_hbm, wu_hbm, wd_hbm, htab_hbm, stab_hbm,
    act_hbm, grad_hbm, h_hbm, du_hbm, a_hbm, df_hbm, small_ref,
    wu, wd, htab, stab, inbuf, recv, sendbuf, deriv, xh1, xh2, rstd,
    hst, pq, u0, u1, acc, low, yst, xst, sums,
    w_sem, t_sem, o_sem, h_sem, send_sem, recv_sem,
):
    first = lax.axis_index("pipe") == 0
    partner = 1 - lax.axis_index("pipe")
    last = blocks - 1

    def wu_copy(b):
        return pltpu.make_async_copy(wu_hbm.at[0, :, pl.ds(b * fb, fb)], wu.at[b], w_sem.at[b])

    def wd_copy(b):
        return pltpu.make_async_copy(wd_hbm.at[0, pl.ds(b * fb, fb), :], wd.at[b], w_sem.at[blocks + b])

    in_copy = pltpu.make_async_copy(in_hbm, inbuf, t_sem.at[0])
    cot_copy = pltpu.make_async_copy(cot_hbm, inbuf, t_sem.at[0])
    htab_copy = pltpu.make_async_copy(htab_hbm, htab, t_sem.at[1])
    stab_copy = pltpu.make_async_copy(stab_hbm, stab, t_sem.at[2])

    @pl.when(first)
    def _():
        in_copy.start()

    htab_copy.start()
    stab_copy.start()
    for b in range(blocks):
        wu_copy(b).start()
        wd_copy(b).start()

    @pl.when(jnp.logical_not(first))
    def _():
        cot_copy.start()

    sums[...] = jnp.zeros_like(sums)

    barrier = pltpu.get_barrier_semaphore()
    pl.semaphore_signal(barrier, inc=1, device_id={"pipe": partner}, device_id_type=pl.DeviceIdType.MESH)
    pl.semaphore_wait(barrier, 1)

    span = rows // CHUNKS

    def chunk_copy(k, c):
        part = pl.ds(c * span, span)
        return pltpu.make_async_remote_copy(
            src_ref=sendbuf.at[k, part],
            dst_ref=recv.at[k, part],
            send_sem=send_sem.at[k, c],
            recv_sem=recv_sem.at[k, c],
            device_id={"pipe": partner},
            device_id_type=pl.DeviceIdType.MESH,
        )

    def act_copy(k):
        return pltpu.make_async_copy(yst, act_hbm.at[0, k], o_sem.at[0])

    def grad_copy(k):
        return pltpu.make_async_copy(xst, grad_hbm.at[0, k], o_sem.at[1])

    def a_copy(k):
        return pltpu.make_async_copy(low, a_hbm.at[k], o_sem.at[2])

    def df_copy(k):
        return pltpu.make_async_copy(low, df_hbm.at[k], o_sem.at[2])

    def h_copy(k, b):
        return pltpu.make_async_copy(hst.at[b], h_hbm.at[b, k], h_sem.at[b])

    def du_copy(k, b):
        return pltpu.make_async_copy(hst.at[b], du_hbm.at[b, k], h_sem.at[b])

    def arrived(k):
        for c in range(CHUNKS):
            chunk_copy(k, c).wait_recv()

    half = rows // 2
    halves = (slice(0, half), slice(half, rows))
    tiles = [slice(r, r + span) for r in range(0, rows, span)]
    g1 = norm_ref[0:1, :]
    b1 = norm_ref[1:2, :]
    g2 = norm_ref[2:3, :]
    b2 = norm_ref[3:4, :]
    bd = norm_ref[4:5, :]

    def normalized(values):
        centered = values - jnp.mean(values, axis=-1, keepdims=True)
        scale = lax.rsqrt(jnp.mean(centered * centered, axis=-1, keepdims=True) + EPS)
        return centered * scale, scale

    def norm_back(grad, gain, unit, scale):
        scaled = grad * gain
        mean_one = jnp.mean(scaled, axis=-1, keepdims=True)
        mean_two = jnp.mean(scaled * unit, axis=-1, keepdims=True)
        return scale * (scaled - mean_one - unit * mean_two)

    def forward(k, step):
        source = plan[k]
        length = bucket[k]
        level = jnp.where(length == rows, 2, jnp.where(length * 2 == rows, 1, 0))

        @pl.when(step == 0)
        def _():
            htab_copy.wait()

        @pl.when(jnp.logical_and(step == 0, first))
        def _():
            in_copy.wait()

        @pl.when(first)
        def _():
            recv[k] = inbuf[source]

        @pl.when(jnp.logical_not(first))
        def _():
            arrived(k)

        pq[0] = dot(recv[k], htab[0]).astype(BF)
        pq[1] = dot(recv[k], htab[1]).astype(BF)

        @pl.when(step == 0)
        def _():
            stab_copy.wait()

        @pl.when(step > 0)
        def _():
            a_copy(k).wait()
            for b in range(blocks):
                h_copy(k, b).wait()

        for part in halves:
            mixed = dot(stab[level, 0, part, :], pq[0]) + dot(stab[level, 1, part, :], pq[1])
            unit, scale = normalized(recv[k, part, :].astype(F32) + mixed)
            xh1[k, part, :] = unit.astype(BF)
            rstd[k, part, 0:1] = scale
            value = unit * g1 + b1
            low[part, :] = value.astype(BF)
            acc[part, :] = value + bd
        a_copy(k).start()

        @pl.when(step == 0)
        def _():
            for b in range(blocks):
                wu_copy(b).wait()
                wd_copy(b).wait()

        def up(b, u):
            u[...] = dot(low[...], wu[b])

        def activate(b, u):
            pre = u[...] + upb_ref[b]
            square = pre * pre
            level_half = 0.5 * jnp.tanh(pre * (TANH_IN + TANH_CUBE * square)) + 0.5
            value = pre * level_half
            slope = level_half + value * (1.0 - level_half) * (2.0 * TANH_IN + 6.0 * TANH_CUBE * square)
            hst[b] = value.astype(BF)
            deriv[k, b] = slope.astype(BF)

        def down(b):
            acc[...] += dot(hst[b], wd[b])

        buffers = (u0, u1)
        up(0, u0)
        for b in range(blocks):
            if b + 1 < blocks:
                up(b + 1, buffers[(b + 1) % 2])
            if b > 0:
                down(b - 1)
            activate(b, buffers[b % 2])
        down(last)
        for b in range(blocks):
            h_copy(k, b).start()

        @pl.when(k > 0)
        def _():
            act_copy(k).wait()

        for c, part in enumerate(tiles):
            unit, scale = normalized(acc[part, :])
            xh2[k, part, :] = unit.astype(BF)
            rstd[k, part, 1:2] = scale
            value = unit * g2 + b2
            yst[part, :] = value

            @pl.when(first)
            def _():
                sendbuf[k, part, :] = value.astype(BF)
                chunk_copy(k, c).start()

        act_copy(k).start()

    def backward(k, step):
        length = bucket[k]
        level = jnp.where(length == rows, 2, jnp.where(length * 2 == rows, 1, 0))

        @pl.when(jnp.logical_and(k == 0, jnp.logical_not(first)))
        def _():
            cot_copy.wait()

        df_copy(k).wait()
        for b in range(blocks):
            du_copy(k, b).wait()

        @pl.when(k > 0)
        def _():
            grad_copy(k).wait()

        @pl.when(first)
        def _():
            arrived(k)
            xst[...] = recv[k].astype(F32)

        @pl.when(jnp.logical_not(first))
        def _():
            xst[...] = inbuf[k].astype(F32)

        for part in tiles:
            grad = xst[part, :]
            unit = xh2[k, part, :].astype(F32)
            back = norm_back(grad, g2, unit, rstd[k, part, 1:2])
            rounded = back.astype(BF)
            low[part, :] = rounded
            acc[part, :] = back
            sums[2] += fold8(grad * unit)
            sums[3] += fold8(grad)
            sums[4] += fold8(rounded.astype(F32))
        df_copy(k).start()

        def up(b, u):
            u[...] = dot_t(low[...], wd[b])

        def activate(b, u):
            rounded = (u[...] * deriv[k, b].astype(F32)).astype(BF)
            hst[b] = rounded
            sums[5 + b] += fold8(rounded.astype(F32))

        def down(b):
            acc[...] += dot_t(hst[b], wu[b])

        buffers = (u0, u1)
        up(0, u0)
        for b in range(blocks):
            if b + 1 < blocks:
                up(b + 1, buffers[(b + 1) % 2])
            if b > 0:
                down(b - 1)
            activate(b, buffers[b % 2])
        down(last)
        for b in range(blocks):
            du_copy(k, b).start()

        for part in tiles:
            grad = acc[part, :]
            unit = xh1[k, part, :].astype(F32)
            back = norm_back(grad, g1, unit, rstd[k, part, 0:1])
            acc[part, :] = back
            recv[k, part, :] = back.astype(BF)
            sums[0] += fold8(grad * unit)
            sums[1] += fold8(grad)
        pq[0] = dot(stab[level, 0], recv[k]).astype(BF)
        pq[1] = dot(stab[level, 1], recv[k]).astype(BF)

        for i, part in enumerate(halves):
            value = acc[part, :] + dot(pq[0, part, :], htab[0]) + dot(pq[1, part, :], htab[1])
            rounded = value.astype(BF)
            xst[part, :] = jnp.where(first, value, rounded.astype(F32))

            @pl.when(jnp.logical_not(first))
            def _():
                sendbuf[k, part, :] = rounded
                for c in range(i * CHUNKS // 2, (i + 1) * CHUNKS // 2):
                    chunk_copy(k, c).start()

        grad_copy(k).start()

    def one(step, carry):
        forwards = jnp.where(first, step < count, lax.rem(step, 2) == 0)
        k = jnp.where(first, lax.rem(step, count), step // 2)

        @pl.when(forwards)
        def _():
            forward(k, step)

        @pl.when(jnp.logical_not(forwards))
        def _():
            backward(k, step)

        return carry

    lax.fori_loop(0, 2 * count, one, 0)

    end = count - 1

    for n in range(5 + blocks):
        small_ref[n : n + 1, :] = jnp.sum(sums[n], axis=0, keepdims=True)
    for n in range(5 + blocks, small_ref.shape[0]):
        small_ref[n : n + 1, :] = jnp.zeros((1, width), F32)
    act_copy(end).wait()
    grad_copy(end).wait()
    df_copy(end).wait()
    for b in range(blocks):
        du_copy(end, b).wait()
    for k in range(count):
        for c in range(CHUNKS):
            chunk_copy(k, c).wait_send()


def run_layers(bucket, plan, norms, up_bias, inputs, cotangent, up_weight, down_weight):
    count, rows, width = inputs.shape
    hidden = up_weight.shape[-1]
    fb = width
    blocks = hidden // fb
    htab = jnp.asarray(hidden_tables(width))
    stab = jnp.asarray(seq_tables(rows))
    any_spec = pl.BlockSpec(memory_space=pl.ANY)
    smem = pl.BlockSpec(memory_space=pltpu.SMEM)
    vmem = pl.BlockSpec(memory_space=pltpu.VMEM)
    shape = jax.ShapeDtypeStruct
    body = functools.partial(layers_kernel, count, rows, width, blocks, fb)
    flops = count * (12 * rows * width * hidden // 1 + 4 * rows * width * (2 * width + 2 * rows))
    return pl.pallas_call(
        body,
        out_shape=(
            shape((1, count, rows, width), F32),
            shape((1, count, rows, width), F32),
            shape((blocks, count, rows, fb), BF),
            shape((blocks, count, rows, fb), BF),
            shape((count, rows, width), BF),
            shape((count, rows, width), BF),
            shape((16, width), F32),
        ),
        in_specs=[smem, smem, vmem, vmem] + [any_spec] * 6,
        out_specs=(any_spec,) * 6 + (vmem,),
        scratch_shapes=[
            pltpu.VMEM((blocks, width, fb), BF),
            pltpu.VMEM((blocks, fb, width), BF),
            pltpu.VMEM((2, width, width), BF),
            pltpu.VMEM((3, 2, rows, rows), BF),
            pltpu.VMEM((count, rows, width), BF),
            pltpu.VMEM((count, rows, width), BF),
            pltpu.VMEM((count, rows, width), BF),
            pltpu.VMEM((count, blocks, rows, fb), BF),
            pltpu.VMEM((count, rows, width), BF),
            pltpu.VMEM((count, rows, width), BF),
            pltpu.VMEM((count, rows, 128), F32),
            pltpu.VMEM((blocks, rows, fb), BF),
            pltpu.VMEM((2, rows, width), BF),
            pltpu.VMEM((rows, fb), F32),
            pltpu.VMEM((rows, fb), F32),
            pltpu.VMEM((rows, width), F32),
            pltpu.VMEM((rows, width), BF),
            pltpu.VMEM((rows, width), F32),
            pltpu.VMEM((rows, width), F32),
            pltpu.VMEM((5 + blocks, 8, width), F32),
            pltpu.SemaphoreType.DMA((2 * blocks,)),
            pltpu.SemaphoreType.DMA((3,)),
            pltpu.SemaphoreType.DMA((3,)),
            pltpu.SemaphoreType.DMA((blocks,)),
            pltpu.SemaphoreType.DMA((count, CHUNKS)),
            pltpu.SemaphoreType.DMA((count, CHUNKS)),
        ],
        compiler_params=pltpu.CompilerParams(
            collective_id=0, has_side_effects=True, vmem_limit_bytes=63 * 2**20
        ),
        cost_estimate=pl.CostEstimate(flops=flops, bytes_accessed=60 * 2**20, transcendentals=0),
    )(bucket, plan, norms, up_bias, inputs, cotangent, up_weight, down_weight, htab, stab)


def per_device(
    inputs, bucket, plan, cotangent, norm1_gain, norm1_bias, up_weight, up_bias,
    down_weight, down_bias, norm2_gain, norm2_bias,
):
    count, rows, width = inputs.shape
    hidden = up_weight.shape[-1]
    norms = jnp.concatenate(
        [norm1_gain, norm1_bias, norm2_gain, norm2_bias, down_bias, jnp.zeros((3, width), F32)]
    )
    activations, input_grad, h, du, a, df, small = run_layers(
        bucket, plan, norms, up_bias.reshape(-1, 1, width), inputs, cotangent, up_weight, down_weight
    )
    up_grad = jnp.einsum("krd,bkrf->dbf", a, du, preferred_element_type=F32).reshape(1, width, hidden)
    down_grad = jnp.einsum("bkrf,krd->bfd", h, df, preferred_element_type=F32).reshape(1, hidden, width)
    up_grad, down_grad, small = lax.psum((up_grad, down_grad, small), "dp")
    blocks = hidden // width
    return (
        activations, input_grad, small[0:1], small[1:2], up_grad,
        small[5 : 5 + blocks].reshape(1, hidden), down_grad, small[4:5], small[2:3], small[3:4],
    )


def solution(mesh):
    row = P("pipe", None)
    weight = P("pipe", None, None)
    tokens = P(None, "dp", None)
    result = P("pipe", None, "dp", None)
    return jax.shard_map(
        per_device,
        mesh=mesh,
        in_specs=(tokens, P(), P(), tokens, row, row, weight, row, weight, row, row, row),
        out_specs=(result, result, row, row, weight, row, weight, row, row, row),
        check_vma=False,
    )
```

time: 1010 us -> 552 us (0.55)
  matrix products: 499 us -> 31.6 us
  Pallas kernels: 0 us -> 143 us
  other arithmetic: 49.3 us -> 0.01 us
  starting transfers between devices: 29.8 us -> 0.04 us
  between operations: 33.5 us -> 14.1 us
  local copies, waits for them, and re-layouts: 51 us -> 33.8 us
  waiting for transfers between devices: 279 us -> 266 us
    dot_general x60 -> x2, matrix products: 499 us -> 31.6 us  [the longest x1 16.1 us: per_device(): jnp.einsum('krd,bkrf->dbf', a, du, preferred_element_type=F32)]
    pallas_call x0 -> x1, Pallas kernels: none -> 143 us  [run_layers(): pl.pallas_call(body, out_shape=(shape((1, count, rows, width), F32), shap...]
    ppermute x8 -> x0, waiting for transfers between devices: 73.3 us -> none  [passed_along(): return lax.ppermute(block, axis, route)]
    psum x1, waiting for transfers between devices: 206 us -> 266 us  [per_device(): up_grad, down_grad, small = lax.psum((up_grad, down_grad, small), 'dp')]
    ppermute x8 -> x0, starting transfers between devices: 29.8 us -> none  [passed_along(): return lax.ppermute(block, axis, route)]
    another operation x3 -> x0, other arithmetic: 17 us -> none
    unnamed x281 -> x18, local copies, waits for them, and re-layouts: 37.8 us -> 22.1 us
    reduce_sum x29 -> x0, other arithmetic: 15.6 us -> none  [the longest x8 7.07 us: layer_norm(): return centered * lax.rsqrt(variance + 1e-06) * gain + offset]
  transfers between devices with their start and end apart: 9 -> 1, of which waited for: 9 -> 1; matrix products, arithmetic and copies ran while one was open for 10% -> 0% of each run, Pallas kernels for 0% -> 0%
where the time goes in v1:
time: 552 us; the launch traced here: 551 us
  waiting for transfers between devices  266 us (48%)
  Pallas kernels  143 us (26%)
  blocking collectives  63.1 us (11%)
  local copies, waits for them, and re-layouts  33.8 us (6%)
  matrix products  31.6 us (6%)
  between operations  14.1 us (3%)
    psum x1, waiting for transfers between devices, per_device(): up_grad, down_grad, small = lax.psum((up_grad, down_grad, small), 'dp')  266 us
    pallas_call x1, Pallas kernels, run_layers(): pl.pallas_call(body, out_shape=(shape((1, count, rows, width), F32), shap...  143 us
    psum x1, blocking collectives, per_device(): up_grad, down_grad, small = lax.psum((up_grad, down_grad, small), 'dp')  63.1 us
    unnamed x18, local copies, waits for them, and re-layouts  22.1 us
    dot_general x1, matrix products, per_device(): jnp.einsum('krd,bkrf->dbf', a, du, preferred_element_type=F32)  16.1 us
    dot_general x1, matrix products, per_device(): jnp.einsum('bkrf,krd->bfd', h, df, preferred_element_type=F32)  15.4 us
  transfers between devices with their start and end apart: 1, of which 1 were waited for; matrix products, arithmetic and copies ran while one was open for 0% of the time, Pallas kernels for 0%

profile of v1, /device:TPU:0, one launch (start us, length us, event | category | flops | bytes accessed | tf_op | source)
XLA Modules:
  0.0 551.4 jit_solution(1837472463473672199)
XLA Ops:
  7.2 0.0 all-reduce.3.cloned.1.call-start
  7.2 1.4 concatenate.3.norm_ref
  8.6 142.8 %shard_map.213 = (f32[1,4,512,768]{3,2,1,0:T(8,128)}, f32[1,4,512,768]{3,2,1,0:T(8,128)}, bf16[4,4,512,768]{3,2,1,0:T(8,128)(2,1)}, bf16[4,4,512,768]{3,2,1,0:T(...) custom-call(s32[4]{0:T(128)} %bucket.1, s32[4]{0:T(128)} %plan.1, ...), custom_call_target="tpu_custom_call" | custom-call | flops 74088185856 | bytes 62914560 | tf_op jit(solution)/shard_map/pallas_call | solution.py:380
  151.5 16.1 %fusion.2 = f32[768,4,768,1]{0,2,3,1:T(8,128)} fusion(bf16[4,4,512,768]{3,2,1,0:T(8,128)(2,1)} %get-tuple-element.21, bf16[4,512,768]{2,1,0:T(8,128)(2,1)} %get-tuple-element.20), kind=kOutput, calls=%fused_computation.2 | convolution fusion | flops 9663676416 | bytes 25165824 | tf_op jit(solution)/shard_map/krd,bkrf->dbf/dot_general | solution.py:440
  167.6 0.0 copy-start.2
  167.6 9.7 %copy.25 = f32[1,768,3072]{2,1,0:T(8,128)} copy(f32[1,768,3072]{1,2,0:T(8,128)} %bitcast.24) | data formatting | bytes 18874368 | tf_op jit(solution)/shard_map/reshape | solution.py:440
  177.3 0.0 copy-done.2
  177.3 15.4 %fusion = f32[4,768,768,1]{2,1,3,0:T(8,128)} fusion(bf16[4,4,512,768]{3,2,1,0:T(8,128)(2,1)} %get-tuple-element.22, bf16[4,512,768]{2,1,0:T(8,128)(2,1)S(1)} %copy-done.2), kind=kOutput, calls=%fused_computation | convolution fusion | flops 9663676416 | bytes 25165824 | tf_op jit(solution)/shard_map/bkrf,krd->bfd/dot_general | solution.py:441
  192.7 0.0 copy-start.1
  192.7 0.0 all-reduce.3.cloned.1.call-update
  192.8 0.8 copy-done.1
  193.5 63.1 %psum.21 = f32[16,768]{1,0:T(8,128)S(1)} all-reduce(f32[16,768]{1,0:T(8,128)S(1)} %copy-done.1), channel_id=1, replica_groups=mesh['pipe'=2,'dp'=16] {'dp'}, use_global_device_ids=true, to_apply=%region_0.0 | all-reduce | flops 12288 | bytes 98304 | tf_op jit(solution)/shard_map/psum | solution.py:442
  256.6 0.6 copy.31
  257.3 0.6 fusion.4
  257.9 266.0 %all-reduce.3.cloned.1.call-done = (f32[1,768,3072]{2,1,0:T(8,128)}, f32[1,3072,768]{2,1,0:T(8,128)}) async-done(((f32[1,768,3072]{2,1,0:T(8,128)}, f32[1,3072,768]{2,1,0:T(8,128)}), (f32[1,768,3072]{2,1,0:T(8,128)}, f32[1,3072,768]{2,1,0:T(8,128)})) %all-reduce.3.cloned.1.call-update) | async-done | bytes 18874384 | tf_op jit(solution)/shard_map/psum | solution.py:442
  523.8 0.0 copy-start
  523.8 6.7 %copy.36 = f32[1,4,512,768]{3,2,1,0:T(8,128)} copy(f32[1,4,512,768]{3,2,1,0:T(8,128)} %get-tuple-element.41) | data formatting | bytes 12582912
  530.6 0.0 slice-start
  530.6 0.0 slice-start.1
  530.6 6.5 %copy.37 = f32[1,4,512,768]{3,2,1,0:T(8,128)} copy(f32[1,4,512,768]{3,2,1,0:T(8,128)} %get-tuple-element.42) | data formatting | bytes 12582912
  537.0 0.0 copy-done
  537.0 0.0 slice-start.2
  537.0 3.7 copy.38
  540.8 0.0 slice-done
  540.8 0.0 slice-done.1
  540.8 0.0 slice-done.2
  540.8 3.7 copy.39
  (3 shorter events, 0.0 us)
Async XLA Ops:
  7.2 516.6 %all-reduce.3.cloned.1.call-start = ((), (), s32[]{:S(2)}) async-start(), calls=%async_computation | async-start | bytes 37748736 | tf_op jit(solution)/shard_map/psum | solution.py:442
  167.6 9.7 %copy-start.2 = (bf16[4,512,768]{2,1,0:T(8,128)(2,1)S(1)}, bf16[4,512,768]{2,1,0:T(8,128)(2,1)}, u32[]{:S(2)}) copy-start(bf16[4,512,768]{2,1,0:T(8,128)(2,1)} %get-tuple-element.23) | copy-start | bytes 9437188
  192.7 0.8 copy-start.1
  523.8 13.2 %copy-start = (f32[1,768,3072]{2,1,0:T(8,128)S(1)}, f32[1,768,3072]{2,1,0:T(8,128)}, u32[]{:S(2)}) copy-start(f32[1,768,3072]{2,1,0:T(8,128)} %get-tuple-element.45) | copy-start | bytes 28311556
  530.6 10.2 %slice-start = ((s8[9437184]{0:T(1024)(128)(4,1)}), s8[4194304]{0:T(1024)(128)(4,1)S(1)}, s32[]{:S(2)}) async-start(s8[9437184]{0:T(1024)(128)(4,1)} %bitcast.21), calls=%async_computation.1 | async-start | bytes 8388608
  530.6 10.2 %slice-start.1 = ((s8[9437184]{0:T(1024)(128)(4,1)}), s8[4194304]{0:T(1024)(128)(4,1)S(1)}, s32[]{:S(2)}) async-start(s8[9437184]{0:T(1024)(128)(4,1)} %bitcast.21), calls=%async_computation.2 | async-start | bytes 8388608
  537.0 3.8 slice-start.2
Sparse Core Ops, SparseCore 0:
  192.9 330.8 all-reduce.2

commit v2 on v1

--- a/solution.py
+++ b/solution.py
@@ -425,6 +425,394 @@
     )(bucket, plan, norms, up_bias, inputs, cotangent, up_weight, down_weight, htab, stab)
 
 
+KINDS = 13
+C1, Y1, CHY, INY, RY, Y2, CHZ, INZ, YZ, RZH, RZF, SY, SZ = range(KINDS)
+RING = 4
+LAG = 7
+
+
+def grads_kernel(
+    dp, count, rows, width, units, wide, per_block,
+    a_hbm, df_hbm, h_hbm, du_hbm, small_ref,
+    out_hbm, small_out,
+    at, abuf, dfb, xb, prod, cur, res, c1in, y1in, chy, iny, chz, inz, yz, sm, smin,
+    in_sem, x_sem, out_sem, send_sem, recv_sem, sm_send, sm_recv,
+):
+    me = lax.axis_index("dp")
+    n = dp // 4
+    core = me % 2
+    side = (me // 2) % 2
+    z = me // 4
+    low = z < n // 2
+    inner = jnp.logical_or(z == n // 2 - 1, z == n // 2)
+    outer = jnp.logical_not(inner)
+    has_out = jnp.logical_and(z > 0, z < n - 1)
+    edge = jnp.logical_not(has_out)
+    toward = jnp.where(low, 4, -4)
+    inward = me + toward
+    outward = me - toward
+    sibling = me + 1 - 2 * core
+    across = me + 2 - 4 * side
+    keep = jnp.where(low, 0, 1)
+    half = units // 2
+    steps = dp.bit_length() - 1
+    home = core * 4
+
+    def x_start(u):
+        slot = u % 3
+        j = u % half
+        block = j // per_block
+        part = pl.ds(pl.multiple_of((j % per_block) * wide, wide), wide)
+
+        @pl.when(u < half)
+        def _():
+            pltpu.make_async_copy(h_hbm.at[block, :, :, part], xb.at[slot], x_sem.at[slot]).start()
+
+        @pl.when(u >= half)
+        def _():
+            pltpu.make_async_copy(du_hbm.at[block, :, :, part], xb.at[slot], x_sem.at[slot]).start()
+
+    def x_wait(u):
+        slot = u % 3
+        pltpu.make_async_copy(h_hbm.at[0, :, :, pl.ds(0, wide)], xb.at[slot], x_sem.at[slot]).wait()
+
+    df_copy = pltpu.make_async_copy(df_hbm, dfb, in_sem.at[0])
+    a_copy = pltpu.make_async_copy(a_hbm, abuf, in_sem.at[1])
+    df_copy.start()
+    x_start(0)
+    x_start(1)
+    a_copy.start()
+
+    def partner(s):
+        return me + 2**s - 2 ** (s + 1) * ((me // 2**s) % 2)
+
+    barrier = pltpu.get_barrier_semaphore()
+    for s in range(steps):
+        pl.semaphore_signal(barrier, inc=1, device_id={"dp": partner(s)}, device_id_type=pl.DeviceIdType.MESH)
+    pl.semaphore_signal(barrier, inc=1, device_id={"dp": inward}, device_id_type=pl.DeviceIdType.MESH)
+
+    @pl.when(has_out)
+    def _():
+        pl.semaphore_signal(barrier, inc=1, device_id={"dp": outward}, device_id_type=pl.DeviceIdType.MESH)
+        pl.semaphore_wait(barrier, steps + 2)
+
+    @pl.when(edge)
+    def _():
+        pl.semaphore_wait(barrier, steps + 1)
+
+    def small_copy(s):
+        return pltpu.make_async_remote_copy(
+            src_ref=sm.at[s], dst_ref=smin.at[s], send_sem=sm_send.at[s], recv_sem=sm_recv.at[s],
+            device_id={"dp": partner(s)}, device_id_type=pl.DeviceIdType.MESH,
+        )
+
+    sm[0] = small_ref[...]
+    small_copy(0).start()
+
+    def message(kind, u, src, dst, target):
+        return pltpu.make_async_remote_copy(
+            src_ref=src, dst_ref=dst, send_sem=send_sem.at[kind, u % RING], recv_sem=recv_sem.at[kind, u],
+            device_id={"dp": target}, device_id_type=pl.DeviceIdType.MESH,
+        )
+
+    def c1(u):
+        return message(C1, u, prod.at[u % RING, pl.ds(4 - home, 4)], c1in.at[u], sibling)
+
+    def y1(u):
+        return message(Y1, u, cur.at[u, 1 - side], y1in.at[u], across)
+
+    def ch_y(u):
+        return message(CHY, u, cur.at[u, side], chy.at[u], inward)
+
+    def in_y(u):
+        return message(INY, u, cur.at[u, side], iny.at[u], inward)
+
+    def r_y(u):
+        return message(RY, u, res.at[u, home + side], res.at[u, home + side], outward)
+
+    def y2(u):
+        return message(Y2, u, res.at[u, home + side], res.at[u, home + side], across)
+
+    def ch_z(u):
+        return message(CHZ, u, cur.at[u, pl.ds(2, 2)], chz.at[u], inward)
+
+    def in_z(u):
+        return message(INZ, u, cur.at[u, 3 - keep], inz.at[u], inward)
+
+    def y_z(u):
+        return message(YZ, u, cur.at[u, 2 + keep], yz.at[u], across)
+
+    def r_zh(u):
+        return message(RZH, u, res.at[u, home + 2 + keep], res.at[u, home + 2 + keep], inward)
+
+    def r_zf(u):
+        return message(RZF, u, res.at[u, pl.ds(home + 2, 2)], res.at[u, pl.ds(home + 2, 2)], outward)
+
+    def s_y(u):
+        return message(SY, u, res.at[u, pl.ds(home, 2)], res.at[u, pl.ds(home, 2)], sibling)
+
+    def s_z(u):
+        return message(SZ, u, res.at[u, pl.ds(home + 2, 2)], res.at[u, pl.ds(home + 2, 2)], sibling)
+
+    def out_copy(u):
+        return pltpu.make_async_copy(res.at[u], out_hbm.at[u], out_sem.at[u % RING])
+
+    def send(make, u):
+        @pl.when(u >= RING)
+        def _():
+            make(u - RING).wait_send()
+
+        make(u).start()
+
+    def plus(left, right):
+        return (left.astype(F32) + right.astype(F32)).astype(BF)
+
+    def compute(u):
+        slot = u % RING
+        x_wait(u)
+
+        @pl.when(u + 2 < units)
+        def _():
+            x_start(u + 2)
+
+        @pl.when(u >= RING)
+        def _():
+            c1(u - RING).wait_send()
+
+        @pl.when(u == 0)
+        def _():
+            df_copy.wait()
+
+        @pl.when(u == half)
+        def _():
+            a_copy.wait()
+            for k in range(count):
+                at[:, k * rows : (k + 1) * rows] = abuf[k].T
+
+        block = xb.at[u % 3]
+
+        @pl.when(u < half)
+        def _():
+            value = lax.dot_general(
+                block[...].reshape(count * rows, wide), dfb[...].reshape(count * rows, width),
+                (((0,), (0,)), ((), ())), preferred_element_type=F32,
+            )
+            value = jnp.concatenate([value[:, t : t + wide] for t in range(0, width, wide)], axis=0)
+            prod[slot] = value.astype(BF).reshape(8, width // 8, wide)
+
+        @pl.when(u >= half)
+        def _():
+            value = dot(at[...], block[...].reshape(count * rows, wide))
+            prod[slot] = value.astype(BF).reshape(8, width // 8, wide)
+
+        c1(u).start()
+
+    def stage1(u):
+        c1(u).wait_recv()
+        cur[u] = plus(prod[u % RING, pl.ds(home, 4)], c1in[u])
+        send(y1, u)
+
+        @pl.when(edge)
+        def _():
+            send(ch_z, u)
+
+    def stage2(u):
+        y1(u).wait_recv()
+        cur[u, side] = plus(cur[u, side], y1in[u])
+
+        @pl.when(edge)
+        def _():
+            send(ch_y, u)
+
+        @pl.when(has_out)
+        def _():
+            ch_z(u).wait_recv()
+            cur[u, 2:4] = plus(cur[u, 2:4], chz[u])
+
+        @pl.when(inner)
+        def _():
+            send(in_z, u)
+
+        @pl.when(jnp.logical_and(outer, has_out))
+        def _():
+            send(ch_z, u)
+
+    def stage3(u):
+        @pl.when(has_out)
+        def _():
+            ch_y(u).wait_recv()
+            cur[u, side] = plus(cur[u, side], chy[u])
+
+        @pl.when(inner)
+        def _():
+            send(in_y, u)
+            in_z(u).wait_recv()
+            cur[u, 2 + keep] = plus(cur[u, 2 + keep], inz[u])
+            send(y_z, u)
+
+        @pl.when(jnp.logical_and(outer, has_out))
+        def _():
+            send(ch_y, u)
+
+    def stage4(u):
+        @pl.when(inner)
+        def _():
+            in_y(u).wait_recv()
+            res[u, home + side] = plus(cur[u, side], iny[u])
+            send(r_y, u)
+            send(y2, u)
+            y_z(u).wait_recv()
+            res[u, home + 2 + keep] = plus(cur[u, 2 + keep], yz[u])
+            send(r_zh, u)
+
+    def stage5(u):
+        @pl.when(outer)
+        def _():
+            r_y(u).wait_recv()
+
+            @pl.when(has_out)
+            def _():
+                send(r_y, u)
+
+            send(y2, u)
+
+        @pl.when(inner)
+        def _():
+            message(
+                RZH, u, res.at[u, home + 3 - keep], res.at[u, home + 3 - keep], inward
+            ).wait_recv()
+            send(r_zf, u)
+            send(s_z, u)
+
+    def stage6(u):
+        message(Y2, u, res.at[u, home + 1 - side], res.at[u, home + 1 - side], across).wait_recv()
+        send(s_y, u)
+
+        @pl.when(outer)
+        def _():
+            r_zf(u).wait_recv()
+
+            @pl.when(has_out)
+            def _():
+                send(r_zf, u)
+
+            send(s_z, u)
+
+    def stage7(u):
+        away = 4 - home
+        message(SY, u, res.at[u, pl.ds(away, 2)], res.at[u, pl.ds(away, 2)], sibling).wait_recv()
+        message(SZ, u, res.at[u, pl.ds(away + 2, 2)], res.at[u, pl.ds(away + 2, 2)], sibling).wait_recv()
+
+        @pl.when(u >= RING)
+        def _():
+            out_copy(u - RING).wait()
+
+        out_copy(u).start()
+
+    stages = (stage1, stage2, stage3, stage4, stage5, stage6, stage7)
+
+    def one(i, carry):
+        @pl.when(i < units)
+        def _():
+            compute(i)
+
+        for lag in range(LAG, 0, -1):
+            u = i - lag
+
+            @pl.when(jnp.logical_and(u >= 0, u < units))
+            def _():
+                stages[lag - 1](u)
+
+        for s in range(steps):
+
+            @pl.when(i == s + 1)
+            def _():
+                small_copy(s).wait_recv()
+                sm[s + 1] = sm[s] + smin[s]
+                if s + 1 < steps:
+                    small_copy(s + 1).start()
+
+        return carry
+
+    lax.fori_loop(0, units + LAG, one, 0)
+
+    small_out[...] = sm[steps]
+    for s in range(steps):
+        small_copy(s).wait_send()
+
+    def drain(u, carry):
+        for make in (c1, y1, y2, s_y, s_z):
+            make(u).wait_send()
+        out_copy(u).wait()
+
+        @pl.when(inner)
+        def _():
+            for make in (in_z, in_y, y_z, r_zh):
+                make(u).wait_send()
+
+        @pl.when(has_out)
+        def _():
+            for make in (r_y, r_zf):
+                make(u).wait_send()
+
+        @pl.when(outer)
+        def _():
+            for make in (ch_y, ch_z):
+                make(u).wait_send()
+
+        return carry
+
+    lax.fori_loop(units - RING, units, drain, 0)
+
+
+def run_grads(dp, a, df, h, du, small):
+    count, rows, width = a.shape
+    blocks, fb = h.shape[0], h.shape[-1]
+    wide = fb // 3
+    half = blocks * 3
+    units = 2 * half
+    steps = dp.bit_length() - 1
+    piece = width // 8
+    any_spec = pl.BlockSpec(memory_space=pl.ANY)
+    vmem = pl.BlockSpec(memory_space=pltpu.VMEM)
+    shape = jax.ShapeDtypeStruct
+    body = functools.partial(grads_kernel, dp, count, rows, width, units, wide, 3)
+    return pl.pallas_call(
+        body,
+        out_shape=(shape((units, 8, piece, wide), BF), shape(small.shape, F32)),
+        in_specs=[any_spec] * 4 + [vmem],
+        out_specs=(any_spec, vmem),
+        scratch_shapes=[
+            pltpu.VMEM((width, count * rows), BF),
+            pltpu.VMEM((count, rows, width), BF),
+            pltpu.VMEM((count, rows, width), BF),
+            pltpu.VMEM((3, count, rows, wide), BF),
+            pltpu.VMEM((RING, 8, piece, wide), BF),
+            pltpu.VMEM((units, 4, piece, wide), BF),
+            pltpu.VMEM((units, 8, piece, wide), BF),
+            pltpu.VMEM((units, 4, piece, wide), BF),
+            pltpu.VMEM((units, piece, wide), BF),
+            pltpu.VMEM((units, piece, wide), BF),
+            pltpu.VMEM((units, piece, wide), BF),
+            pltpu.VMEM((units, 2, piece, wide), BF),
+            pltpu.VMEM((units, piece, wide), BF),
+            pltpu.VMEM((units, piece, wide), BF),
+            pltpu.VMEM((steps + 1,) + small.shape, F32),
+            pltpu.VMEM((steps,) + small.shape, F32),
+            pltpu.SemaphoreType.DMA((2,)),
+            pltpu.SemaphoreType.DMA((3,)),
+            pltpu.SemaphoreType.DMA((RING,)),
+            pltpu.SemaphoreType.DMA((KINDS, RING)),
+            pltpu.SemaphoreType.DMA((KINDS, units)),
+            pltpu.SemaphoreType.DMA((steps,)),
+            pltpu.SemaphoreType.DMA((steps,)),
+        ],
+        compiler_params=pltpu.CompilerParams(
+            collective_id=1, has_side_effects=True, vmem_limit_bytes=60 * 2**20
+        ),
+    )(a, df, h, du, small)
+
+
 def per_device(
     inputs, bucket, plan, cotangent, norm1_gain, norm1_bias, up_weight, up_bias,
     down_weight, down_bias, norm2_gain, norm2_bias,
@@ -437,9 +825,11 @@
     activations, input_grad, h, du, a, df, small = run_layers(
         bucket, plan, norms, up_bias.reshape(-1, 1, width), inputs, cotangent, up_weight, down_weight
     )
-    up_grad = jnp.einsum("krd,bkrf->dbf", a, du, preferred_element_type=F32).reshape(1, width, hidden)
-    down_grad = jnp.einsum("bkrf,krd->bfd", h, df, preferred_element_type=F32).reshape(1, hidden, width)
-    up_grad, down_grad, small = lax.psum((up_grad, down_grad, small), "dp")
+    total, small = run_grads(lax.axis_size("dp"), a, df, h, du, small)
+    units, wide = total.shape[0], total.shape[-1]
+    total = total.reshape(2, units // 2, width // wide, wide, wide)
+    down_grad = total[0].transpose(0, 2, 1, 3).reshape(1, hidden, width).astype(F32)
+    up_grad = total[1].transpose(1, 2, 0, 3).reshape(1, width, hidden).astype(F32)
     blocks = hidden // width
     return (
         activations, input_grad, small[0:1], small[1:2], up_grad,

time: 552 us -> 348 us (0.63)
  waiting for transfers between devices: 266 us -> 0 us
  Pallas kernels: 143 us -> 274 us
  blocking collectives: 63.1 us -> 0 us
  local copies, waits for them, and re-layouts: 33.8 us -> 71.7 us
  matrix products: 31.6 us -> 0 us
  between operations: 14.1 us -> 0.68 us
    psum x1 -> x0, waiting for transfers between devices: 266 us -> none  [per_device(): up_grad, down_grad, small = lax.psum((up_grad, down_grad, small), 'dp')]
    pallas_call x0 -> x1, Pallas kernels: none -> 131 us  [run_grads(): pl.pallas_call(body, out_shape=(shape((units, 8, piece, wide), BF), shape...]
    psum x1 -> x0, blocking collectives: 63.1 us -> none  [per_device(): up_grad, down_grad, small = lax.psum((up_grad, down_grad, small), 'dp')]
    convert_element_type x0 -> x4, local copies, waits for them, and re-layouts: none -> 40.2 us  [the longest x2 20.9 us: per_device(): total[0].transpose(0, 2, 1, 3).reshape(1, hidden, width).astype(F32)]
    dot_general x2 -> x0, matrix products: 31.6 us -> none  [the longest x1 16.1 us: per_device(): jnp.einsum('krd,bkrf->dbf', a, du, preferred_element_type=F32)]
    reshape x1 -> x0, local copies, waits for them, and re-layouts: 9.73 us -> none  [per_device(): jnp.einsum('krd,bkrf->dbf', a, du, preferred_element_type=F32)]
    slice x0 -> x1, local copies, waits for them, and re-layouts: none -> 7.1 us  [per_device(): total[0].transpose(0, 2, 1, 3).reshape(1, hidden, width).astype(F32)]
    unnamed x18 -> x7, local copies, waits for them, and re-layouts: 22.1 us -> 22.4 us
  transfers between devices with their start and end apart: 1 -> 0, of which waited for: 1 -> 0; matrix products, arithmetic and copies ran while one was open for 0% -> 0% of each run, Pallas kernels for 0% -> 0%
where the time goes in v2:
time: 348 us; the launch traced here: 347 us
  Pallas kernels  274 us (79%)
  local copies, waits for them, and re-layouts  71.7 us (21%)
    pallas_call x1, Pallas kernels, run_layers(): pl.pallas_call(body, out_shape=(shape((1, count, rows, width), F32), shap...  143 us
    pallas_call x1, Pallas kernels, run_grads(): pl.pallas_call(body, out_shape=(shape((units, 8, piece, wide), BF), shape...  131 us
    unnamed x7, local copies, waits for them, and re-layouts  22.4 us
    convert_element_type x2, local copies, waits for them, and re-layouts, per_device(): total[0].transpose(0, 2, 1, 3).reshape(1, hidden, width).astype(F32)  20.9 us
    convert_element_type x2, local copies, waits for them, and re-layouts, per_device(): total[1].transpose(1, 2, 0, 3).reshape(1, width, hidden).astype(F32)  19.3 us
    slice x1, local copies, waits for them, and re-layouts, per_device(): total[0].transpose(0, 2, 1, 3).reshape(1, hidden, width).astype(F32)  7.1 us

profile of v2, /device:TPU:0, one launch (start us, length us, event | category | flops | bytes accessed | tf_op | source)
XLA Modules:
  0.0 346.6 jit_solution(3275028598261699421)
XLA Ops:
  0.7 1.4 concatenate.3.norm_ref
  2.0 142.8 %shard_map.213 = (f32[1,4,512,768]{3,2,1,0:T(8,128)}, f32[1,4,512,768]{3,2,1,0:T(8,128)}, bf16[4,4,512,768]{3,2,1,0:T(8,128)(2,1)}, bf16[4,4,512,768]{3,2,1,0:T(...) custom-call(s32[4]{0:T(128)} %bucket.1, s32[4]{0:T(128)} %plan.1, ...), custom_call_target="tpu_custom_call" | custom-call | flops 74088185856 | bytes 62914560 | tf_op jit(solution)/shard_map/pallas_call | solution.py:380
  144.8 131.4 %shard_map.214 = (bf16[24,8,96,256]{3,2,1,0:T(8,128)(2,1)}, f32[16,768]{1,0:T(8,128)}) custom-call(bf16[4,512,768]{2,1,0:T(8,128)(2,1)} %get-tuple-element.21.a_hbm, bf16[4,512,768]{2,1,0:T(8,128)(2,1)} %get-tuple-element.22.df_hbm, bf16[4,4,512,768]{3,2,1,0:T(8,128)(2,1)} %get-tuple-element.23.h_hbm, bf16[4,4,512,768]{3,2,1,0:T(8,128)(2,1)} %get-tuple-element.24.du_hbm, ...), custom_call_target="tpu_custom_call" | custom-call | tf_op jit(solution)/shard_map/pallas_call | solution.py:780
  276.3 0.0 copy-start
  276.3 7.1 %fusion = (bf16[12,8,96,256]{3,2,1,0:T(8,128)(2,1)}, bf16[12,8,96,256]{3,2,1,0:T(8,128)(2,1)S(1)}) fusion(bf16[24,8,96,256]{3,2,1,0:T(8,128)(2,1)} %get-tuple-element.27), kind=kLoop, calls=%fused_computation.2 | loop fusion | bytes 18874368 | tf_op jit(solution)/shard_map/slice | solution.py:831
  283.4 0.0 copy-done
  283.4 0.6 fusion.1
  284.0 0.6 copy.29
  284.6 7.5 %copy.31 = f32[12,3,256,256]{3,0,2,1:T(8,128)} copy(bf16[12,3,256,256]{3,2,1,0:T(8,128)(2,1)S(1)} %bitcast.18) | data formatting | bytes 14155776 | tf_op jit(solution)/shard_map/convert_element_type | solution.py:832
  292.1 11.8 %reshape.67 = f32[1,768,3072]{2,1,0:T(8,128)} reshape(f32[3,256,12,256]{3,2,1,0:T(8,128)} %bitcast.15) | data formatting | bytes 18874368 | tf_op jit(solution)/shard_map/convert_element_type | solution.py:832
  304.0 9.1 %copy.27 = f32[12,3,256,256]{2,0,3,1:T(8,128)} copy(bf16[12,3,256,256]{3,2,1,0:T(8,128)(2,1)} %bitcast.17) | data formatting | bytes 14155776 | tf_op jit(solution)/shard_map/convert_element_type | solution.py:831
  313.0 11.8 %reshape.68 = f32[1,3072,768]{1,2,0:T(8,128)} reshape(f32[12,256,3,256]{1,0,3,2:T(8,128)} %bitcast.16) | data formatting | bytes 18874368 | tf_op jit(solution)/shard_map/convert_element_type | solution.py:831
  324.9 9.6 %copy.28 = f32[1,3072,768]{2,1,0:T(8,128)} copy(f32[1,3072,768]{1,2,0:T(8,128)} %reshape.68) | data formatting | bytes 18874368
  334.4 6.1 %copy.34 = f32[1,4,512,768]{3,2,1,0:T(8,128)} copy(f32[1,4,512,768]{3,2,1,0:T(8,128)} %get-tuple-element.55) | data formatting | bytes 12582912
  340.5 6.1 %copy.35 = f32[1,4,512,768]{3,2,1,0:T(8,128)} copy(f32[1,4,512,768]{3,2,1,0:T(8,128)} %get-tuple-element.56) | data formatting | bytes 12582912
  (2 shorter events, 0.0 us)
Async XLA Ops:
  276.3 7.1 %copy-start = (f32[16,768]{1,0:T(8,128)S(1)}, f32[16,768]{1,0:T(8,128)}, u32[]{:S(2)}) copy-start(f32[16,768]{1,0:T(8,128)} %get-tuple-element.26) | copy-start | bytes 147460

commit v3 on v2

--- a/solution.py
+++ b/solution.py
@@ -60,7 +60,7 @@
     bucket, plan, norm_ref, upb_ref, in_hbm, cot_hbm, wu_hbm, wd_hbm, htab_hbm, stab_hbm,
     act_hbm, grad_hbm, h_hbm, du_hbm, a_hbm, df_hbm, small_ref,
     wu, wd, htab, stab, inbuf, recv, sendbuf, deriv, xh1, xh2, rstd,
-    hst, pq, u0, u1, acc, low, yst, xst, sums,
+    hst, pq, u0, u1, acc, alow, dlow, yst, xst, sums,
     w_sem, t_sem, o_sem, h_sem, send_sem, recv_sem,
 ):
     first = lax.axis_index("pipe") == 0
@@ -118,10 +118,10 @@
         return pltpu.make_async_copy(xst, grad_hbm.at[0, k], o_sem.at[1])
 
     def a_copy(k):
-        return pltpu.make_async_copy(low, a_hbm.at[k], o_sem.at[2])
+        return pltpu.make_async_copy(alow, a_hbm.at[k], o_sem.at[2])
 
     def df_copy(k):
-        return pltpu.make_async_copy(low, df_hbm.at[k], o_sem.at[2])
+        return pltpu.make_async_copy(dlow, df_hbm.at[k], o_sem.at[3])
 
     def h_copy(k, b):
         return pltpu.make_async_copy(hst.at[b], h_hbm.at[b, k], h_sem.at[b])
@@ -129,13 +129,19 @@
     def du_copy(k, b):
         return pltpu.make_async_copy(hst.at[b], du_hbm.at[b, k], h_sem.at[b])
 
-    def arrived(k):
-        for c in range(CHUNKS):
+    def arrived(k, i):
+        for c in range(i * CHUNKS // 2, (i + 1) * CHUNKS // 2):
             chunk_copy(k, c).wait_recv()
+
+    def leave(k, i):
+        for c in range(i * CHUNKS // 2, (i + 1) * CHUNKS // 2):
+            chunk_copy(k, c).start()
 
     half = rows // 2
     halves = (slice(0, half), slice(half, rows))
-    tiles = [slice(r, r + span) for r in range(0, rows, span)]
+    tiles = [[slice(r, r + span) for r in range(h.start, h.stop, span)] for h in halves]
+    order = [(i, b) for i in range(2) for b in range(blocks)]
+    buffers = (u0, u1)
     g1 = norm_ref[0:1, :]
     b1 = norm_ref[1:2, :]
     g2 = norm_ref[2:3, :]
@@ -153,6 +159,22 @@
         mean_two = jnp.mean(scaled * unit, axis=-1, keepdims=True)
         return scale * (scaled - mean_one - unit * mean_two)
 
+    def pipelined(up, activate, down, before, after):
+        before(0)
+        up(*order[0], u0)
+        for n, (i, b) in enumerate(order):
+            if n + 1 < len(order):
+                if order[n + 1][1] == 0:
+                    before(order[n + 1][0])
+                up(*order[n + 1], buffers[(n + 1) % 2])
+            if n > 0:
+                down(*order[n - 1])
+            activate(i, b, buffers[n % 2])
+            if n > 0 and order[n - 1][1] == last:
+                after(order[n - 1][0])
+        down(*order[-1])
+        after(1)
+
     def forward(k, step):
         source = plan[k]
         length = bucket[k]
@@ -170,12 +192,14 @@
         def _():
             recv[k] = inbuf[source]
 
-        @pl.when(jnp.logical_not(first))
-        def _():
-            arrived(k)
-
-        pq[0] = dot(recv[k], htab[0]).astype(BF)
-        pq[1] = dot(recv[k], htab[1]).astype(BF)
+        for i, part in enumerate(halves):
+
+            @pl.when(jnp.logical_not(first))
+            def _():
+                arrived(k, i)
+
+            pq[0, part] = dot(recv[k, part], htab[0]).astype(BF)
+            pq[1, part] = dot(recv[k, part], htab[1]).astype(BF)
 
         @pl.when(step == 0)
         def _():
@@ -183,9 +207,12 @@
 
         @pl.when(step > 0)
         def _():
-            a_copy(k).wait()
             for b in range(blocks):
                 h_copy(k, b).wait()
+
+        @pl.when(k > 0)
+        def _():
+            a_copy(k).wait()
 
         for part in halves:
             mixed = dot(stab[level, 0, part, :], pq[0]) + dot(stab[level, 1, part, :], pq[1])
@@ -193,7 +220,7 @@
             xh1[k, part, :] = unit.astype(BF)
             rstd[k, part, 0:1] = scale
             value = unit * g1 + b1
-            low[part, :] = value.astype(BF)
+            alow[part, :] = value.astype(BF)
             acc[part, :] = value + bd
         a_copy(k).start()
 
@@ -203,49 +230,44 @@
                 wu_copy(b).wait()
                 wd_copy(b).wait()
 
-        def up(b, u):
-            u[...] = dot(low[...], wu[b])
-
-        def activate(b, u):
+        @pl.when(k > 0)
+        def _():
+            act_copy(k).wait()
+
+        def up(i, b, u):
+            u[...] = dot(alow[halves[i], :], wu[b])
+
+        def activate(i, b, u):
             pre = u[...] + upb_ref[b]
             square = pre * pre
             level_half = 0.5 * jnp.tanh(pre * (TANH_IN + TANH_CUBE * square)) + 0.5
             value = pre * level_half
             slope = level_half + value * (1.0 - level_half) * (2.0 * TANH_IN + 6.0 * TANH_CUBE * square)
-            hst[b] = value.astype(BF)
-            deriv[k, b] = slope.astype(BF)
-
-        def down(b):
-            acc[...] += dot(hst[b], wd[b])
-
-        buffers = (u0, u1)
-        up(0, u0)
-        for b in range(blocks):
-            if b + 1 < blocks:
-                up(b + 1, buffers[(b + 1) % 2])
-            if b > 0:
-                down(b - 1)
-            activate(b, buffers[b % 2])
-        down(last)
+            hst[b, halves[i], :] = value.astype(BF)
+            deriv[k, b, halves[i], :] = slope.astype(BF)
+
+        def down(i, b):
+            acc[halves[i], :] += dot(hst[b, halves[i], :], wd[b])
+
+        def before(i):
+            pass
+
+        def after(i):
+            for part in tiles[i]:
+                unit, scale = normalized(acc[part, :])
+                xh2[k, part, :] = unit.astype(BF)
+                rstd[k, part, 1:2] = scale
+                value = unit * g2 + b2
+                yst[part, :] = value
+                sendbuf[k, part, :] = value.astype(BF)
+
+            @pl.when(first)
+            def _():
+                leave(k, i)
+
+        pipelined(up, activate, down, before, after)
         for b in range(blocks):
             h_copy(k, b).start()
-
-        @pl.when(k > 0)
-        def _():
-            act_copy(k).wait()
-
-        for c, part in enumerate(tiles):
-            unit, scale = normalized(acc[part, :])
-            xh2[k, part, :] = unit.astype(BF)
-            rstd[k, part, 1:2] = scale
-            value = unit * g2 + b2
-            yst[part, :] = value
-
-            @pl.when(first)
-            def _():
-                sendbuf[k, part, :] = value.astype(BF)
-                chunk_copy(k, c).start()
-
         act_copy(k).start()
 
     def backward(k, step):
@@ -256,66 +278,61 @@
         def _():
             cot_copy.wait()
 
-        df_copy(k).wait()
-        for b in range(blocks):
-            du_copy(k, b).wait()
+        @pl.when(first)
+        def _():
+            for c in range(CHUNKS):
+                chunk_copy(k, c).wait_send()
 
         @pl.when(k > 0)
         def _():
+            df_copy(k).wait()
             grad_copy(k).wait()
 
-        @pl.when(first)
-        def _():
-            arrived(k)
-            xst[...] = recv[k].astype(F32)
-
-        @pl.when(jnp.logical_not(first))
-        def _():
-            xst[...] = inbuf[k].astype(F32)
-
-        for part in tiles:
-            grad = xst[part, :]
-            unit = xh2[k, part, :].astype(F32)
-            back = norm_back(grad, g2, unit, rstd[k, part, 1:2])
-            rounded = back.astype(BF)
-            low[part, :] = rounded
-            acc[part, :] = back
-            sums[2] += fold8(grad * unit)
-            sums[3] += fold8(grad)
-            sums[4] += fold8(rounded.astype(F32))
+        def before(i):
+            @pl.when(first)
+            def _():
+                arrived(k, i)
+
+            for part in tiles[i]:
+                grad = jnp.where(first, recv[k, part, :], inbuf[k, part, :]).astype(F32)
+                unit = xh2[k, part, :].astype(F32)
+                back = norm_back(grad, g2, unit, rstd[k, part, 1:2])
+                rounded = back.astype(BF)
+                dlow[part, :] = rounded
+                acc[part, :] = back
+                sums[2] += fold8(grad * unit)
+                sums[3] += fold8(grad)
+                sums[4] += fold8(rounded.astype(F32))
+            if i == 0:
+                for b in range(blocks):
+                    du_copy(k, b).wait()
+
+        def up(i, b, u):
+            u[...] = dot_t(dlow[halves[i], :], wd[b])
+
+        def activate(i, b, u):
+            rounded = (u[...] * deriv[k, b, halves[i], :].astype(F32)).astype(BF)
+            hst[b, halves[i], :] = rounded
+            sums[5 + b] += fold8(rounded.astype(F32))
+
+        def down(i, b):
+            acc[halves[i], :] += dot_t(hst[b, halves[i], :], wu[b])
+
+        def after(i):
+            for part in tiles[i]:
+                grad = acc[part, :]
+                unit = xh1[k, part, :].astype(F32)
+                back = norm_back(grad, g1, unit, rstd[k, part, 0:1])
+                acc[part, :] = back
+                recv[k, part, :] = back.astype(BF)
+                sums[0] += fold8(grad * unit)
+                sums[1] += fold8(grad)
+
+        pipelined(up, activate, down, before, after)
         df_copy(k).start()
-
-        def up(b, u):
-            u[...] = dot_t(low[...], wd[b])
-
-        def activate(b, u):
-            rounded = (u[...] * deriv[k, b].astype(F32)).astype(BF)
-            hst[b] = rounded
-            sums[5 + b] += fold8(rounded.astype(F32))
-
-        def down(b):
-            acc[...] += dot_t(hst[b], wu[b])
-
-        buffers = (u0, u1)
-        up(0, u0)
-        for b in range(blocks):
-            if b + 1 < blocks:
-                up(b + 1, buffers[(b + 1) % 2])
-            if b > 0:
-                down(b - 1)
-            activate(b, buffers[b % 2])
-        down(last)
         for b in range(blocks):
             du_copy(k, b).start()
 
-        for part in tiles:
-            grad = acc[part, :]
-            unit = xh1[k, part, :].astype(F32)
-            back = norm_back(grad, g1, unit, rstd[k, part, 0:1])
-            acc[part, :] = back
-            recv[k, part, :] = back.astype(BF)
-            sums[0] += fold8(grad * unit)
-            sums[1] += fold8(grad)
         pq[0] = dot(stab[level, 0], recv[k]).astype(BF)
         pq[1] = dot(stab[level, 1], recv[k]).astype(BF)
 
@@ -323,12 +340,11 @@
             value = acc[part, :] + dot(pq[0, part, :], htab[0]) + dot(pq[1, part, :], htab[1])
             rounded = value.astype(BF)
             xst[part, :] = jnp.where(first, value, rounded.astype(F32))
+            sendbuf[k, part, :] = rounded
 
             @pl.when(jnp.logical_not(first))
             def _():
-                sendbuf[k, part, :] = rounded
-                for c in range(i * CHUNKS // 2, (i + 1) * CHUNKS // 2):
-                    chunk_copy(k, c).start()
+                leave(k, i)
 
         grad_copy(k).start()
 
@@ -356,12 +372,16 @@
         small_ref[n : n + 1, :] = jnp.zeros((1, width), F32)
     act_copy(end).wait()
     grad_copy(end).wait()
+    a_copy(end).wait()
     df_copy(end).wait()
     for b in range(blocks):
         du_copy(end, b).wait()
-    for k in range(count):
-        for c in range(CHUNKS):
-            chunk_copy(k, c).wait_send()
+
+    @pl.when(jnp.logical_not(first))
+    def _():
+        for k in range(count):
+            for c in range(CHUNKS):
+                chunk_copy(k, c).wait_send()
 
 
 def run_layers(bucket, plan, norms, up_bias, inputs, cotangent, up_weight, down_weight):
@@ -404,16 +424,17 @@
             pltpu.VMEM((count, rows, 128), F32),
             pltpu.VMEM((blocks, rows, fb), BF),
             pltpu.VMEM((2, rows, width), BF),
-            pltpu.VMEM((rows, fb), F32),
-            pltpu.VMEM((rows, fb), F32),
+            pltpu.VMEM((rows // 2, fb), F32),
+            pltpu.VMEM((rows // 2, fb), F32),
             pltpu.VMEM((rows, width), F32),
+            pltpu.VMEM((rows, width), BF),
             pltpu.VMEM((rows, width), BF),
             pltpu.VMEM((rows, width), F32),
             pltpu.VMEM((rows, width), F32),
             pltpu.VMEM((5 + blocks, 8, width), F32),
             pltpu.SemaphoreType.DMA((2 * blocks,)),
             pltpu.SemaphoreType.DMA((3,)),
-            pltpu.SemaphoreType.DMA((3,)),
+            pltpu.SemaphoreType.DMA((4,)),
             pltpu.SemaphoreType.DMA((blocks,)),
             pltpu.SemaphoreType.DMA((count, CHUNKS)),
             pltpu.SemaphoreType.DMA((count, CHUNKS)),
@@ -428,14 +449,14 @@
 KINDS = 13
 C1, Y1, CHY, INY, RY, Y2, CHZ, INZ, YZ, RZH, RZF, SY, SZ = range(KINDS)
 RING = 4
-LAG = 7
+LAGS = (1, 3, 5, 7, 9, 11, 12)
 
 
 def grads_kernel(
     dp, count, rows, width, units, wide, per_block,
     a_hbm, df_hbm, h_hbm, du_hbm, small_ref,
-    out_hbm, small_out,
-    at, abuf, dfb, xb, prod, cur, res, c1in, y1in, chy, iny, chz, inz, yz, sm, smin,
+    down_hbm, up_hbm, small_out,
+    at, abuf, dfb, xb, prod, cur, res, stage, c1in, y1in, chy, iny, chz, inz, yz, sm, smin,
     in_sem, x_sem, out_sem, send_sem, recv_sem, sm_send, sm_recv,
 ):
     me = lax.axis_index("dp")
@@ -554,8 +575,19 @@
     def s_z(u):
         return message(SZ, u, res.at[u, pl.ds(home + 2, 2)], res.at[u, pl.ds(home + 2, 2)], sibling)
 
-    def out_copy(u):
-        return pltpu.make_async_copy(res.at[u], out_hbm.at[u], out_sem.at[u % RING])
+    def down_copy(u, t):
+        part = pl.ds(pl.multiple_of(u * wide, wide), wide)
+        return pltpu.make_async_copy(
+            stage.at[u % 2, pl.ds(t * wide, wide)], down_hbm.at[0, part, pl.ds(t * wide, wide)],
+            out_sem.at[u % 2, t],
+        )
+
+    def up_copy(u, t, slot):
+        part = pl.ds(pl.multiple_of((u - half) * wide, wide), wide)
+        return pltpu.make_async_copy(
+            stage.at[slot, pl.ds(t * wide, wide)], up_hbm.at[0, pl.ds(t * wide, wide), part],
+            out_sem.at[slot, t],
+        )
 
     def send(make, u):
         @pl.when(u >= RING)
@@ -703,11 +735,22 @@
         message(SY, u, res.at[u, pl.ds(away, 2)], res.at[u, pl.ds(away, 2)], sibling).wait_recv()
         message(SZ, u, res.at[u, pl.ds(away + 2, 2)], res.at[u, pl.ds(away + 2, 2)], sibling).wait_recv()
 
-        @pl.when(u >= RING)
-        def _():
-            out_copy(u - RING).wait()
-
-        out_copy(u).start()
+        @pl.when(u >= 2)
+        def _():
+            for t in range(width // wide):
+                up_copy(half, t, u % 2).wait()
+
+        stage[u % 2] = res[u].reshape(width, wide).astype(F32)
+
+        @pl.when(u < half)
+        def _():
+            for t in range(width // wide):
+                down_copy(u, t).start()
+
+        @pl.when(u >= half)
+        def _():
+            for t in range(width // wide):
+                up_copy(u, t, u % 2).start()
 
     stages = (stage1, stage2, stage3, stage4, stage5, stage6, stage7)
 
@@ -716,12 +759,12 @@
         def _():
             compute(i)
 
-        for lag in range(LAG, 0, -1):
+        for work, lag in reversed(list(zip(stages, LAGS))):
             u = i - lag
 
             @pl.when(jnp.logical_and(u >= 0, u < units))
             def _():
-                stages[lag - 1](u)
+                work(u)
 
         for s in range(steps):
 
@@ -734,7 +777,7 @@
 
         return carry
 
-    lax.fori_loop(0, units + LAG, one, 0)
+    lax.fori_loop(0, units + LAGS[-1], one, 0)
 
     small_out[...] = sm[steps]
     for s in range(steps):
@@ -743,7 +786,6 @@
     def drain(u, carry):
         for make in (c1, y1, y2, s_y, s_z):
             make(u).wait_send()
-        out_copy(u).wait()
 
         @pl.when(inner)
         def _():
@@ -763,6 +805,9 @@
         return carry
 
     lax.fori_loop(units - RING, units, drain, 0)
+    for slot in range(2):
+        for t in range(width // wide):
+            up_copy(half, t, slot).wait()
 
 
 def run_grads(dp, a, df, h, du, small):
@@ -773,15 +818,16 @@
     units = 2 * half
     steps = dp.bit_length() - 1
     piece = width // 8
+    hidden = blocks * fb
     any_spec = pl.BlockSpec(memory_space=pl.ANY)
     vmem = pl.BlockSpec(memory_space=pltpu.VMEM)
     shape = jax.ShapeDtypeStruct
     body = functools.partial(grads_kernel, dp, count, rows, width, units, wide, 3)
     return pl.pallas_call(
         body,
-        out_shape=(shape((units, 8, piece, wide), BF), shape(small.shape, F32)),
+        out_shape=(shape((1, hidden, width), F32), shape((1, width, hidden), F32), shape(small.shape, F32)),
         in_specs=[any_spec] * 4 + [vmem],
-        out_specs=(any_spec, vmem),
+        out_specs=(any_spec, any_spec, vmem),
         scratch_shapes=[
             pltpu.VMEM((width, count * rows), BF),
             pltpu.VMEM((count, rows, width), BF),
@@ -790,6 +836,7 @@
             pltpu.VMEM((RING, 8, piece, wide), BF),
             pltpu.VMEM((units, 4, piece, wide), BF),
             pltpu.VMEM((units, 8, piece, wide), BF),
+            pltpu.VMEM((2, width, wide), F32),
             pltpu.VMEM((units, 4, piece, wide), BF),
             pltpu.VMEM((units, piece, wide), BF),
             pltpu.VMEM((units, piece, wide), BF),
@@ -801,7 +848,7 @@
             pltpu.VMEM((steps,) + small.shape, F32),
             pltpu.SemaphoreType.DMA((2,)),
             pltpu.SemaphoreType.DMA((3,)),
-            pltpu.SemaphoreType.DMA((RING,)),
+            pltpu.SemaphoreType.DMA((2, 3)),
             pltpu.SemaphoreType.DMA((KINDS, RING)),
             pltpu.SemaphoreType.DMA((KINDS, units)),
             pltpu.SemaphoreType.DMA((steps,)),
@@ -825,11 +872,7 @@
     activations, input_grad, h, du, a, df, small = run_layers(
         bucket, plan, norms, up_bias.reshape(-1, 1, width), inputs, cotangent, up_weight, down_weight
     )
-    total, small = run_grads(lax.axis_size("dp"), a, df, h, du, small)
-    units, wide = total.shape[0], total.shape[-1]
-    total = total.reshape(2, units // 2, width // wide, wide, wide)
-    down_grad = total[0].transpose(0, 2, 1, 3).reshape(1, hidden, width).astype(F32)
-    up_grad = total[1].transpose(1, 2, 0, 3).reshape(1, width, hidden).astype(F32)
+    down_grad, up_grad, small = run_grads(lax.axis_size("dp"), a, df, h, du, small)
     blocks = hidden // width
     return (
         activations, input_grad, small[0:1], small[1:2], up_grad,

time: 348 us -> 277 us (0.80)
  local copies, waits for them, and re-layouts: 71.7 us -> 25.1 us
  Pallas kernels: 274 us -> 250 us
    convert_element_type x4 -> x0, local copies, waits for them, and re-layouts: 40.2 us -> none  [the longest x2 20.9 us: per_device(): total[0].transpose(0, 2, 1, 3).reshape(1, hidden, width).astype(F32)]
    pallas_call x1, Pallas kernels: 131 us -> 112 us  [run_grads(): pl.pallas_call(body, out_shape=(shape((1, hidden, width), F32), shape((1,...]
    slice x1 -> x0, local copies, waits for them, and re-layouts: 7.1 us -> none  [per_device(): total[0].transpose(0, 2, 1, 3).reshape(1, hidden, width).astype(F32)]
    pallas_call x1, Pallas kernels: 143 us -> 138 us  [run_layers(): pl.pallas_call(body, out_shape=(shape((1, count, rows, width), F32), shap...]
    unnamed x7 -> x14, local copies, waits for them, and re-layouts: 22.4 us -> 22.1 us
where the time goes in v3:
time: 277 us; the launch traced here: 276 us
  Pallas kernels  250 us (90%)
  local copies, waits for them, and re-layouts  25.1 us (9%)
    pallas_call x1, Pallas kernels, run_layers(): pl.pallas_call(body, out_shape=(shape((1, count, rows, width), F32), shap...  138 us
    pallas_call x1, Pallas kernels, run_grads(): pl.pallas_call(body, out_shape=(shape((1, hidden, width), F32), shape((1,...  112 us
    unnamed x14, local copies, waits for them, and re-layouts  22.1 us

profile of v3, /device:TPU:0, one launch (start us, length us, event | category | flops | bytes accessed | tf_op | source)
XLA Modules:
  0.0 276.1 jit_solution(15483260940789835072)
XLA Ops:
  0.7 1.4 concatenate.3.norm_ref
  2.0 138.4 %shard_map.213 = (f32[1,4,512,768]{3,2,1,0:T(8,128)}, f32[1,4,512,768]{3,2,1,0:T(8,128)}, bf16[4,4,512,768]{3,2,1,0:T(8,128)(2,1)}, bf16[4,4,512,768]{3,2,1,0:T(...) custom-call(s32[4]{0:T(128)} %bucket.1, s32[4]{0:T(128)} %plan.1, ...), custom_call_target="tpu_custom_call" | custom-call | flops 74088185856 | bytes 62914560 | tf_op jit(solution)/shard_map/pallas_call | solution.py:400
  140.4 112.0 %shard_map.214 = (f32[1,3072,768]{2,1,0:T(8,128)}, f32[1,768,3072]{2,1,0:T(8,128)}, f32[16,768]{1,0:T(8,128)}) custom-call(bf16[4,512,768]{2,1,0:T(8,128)(2,1)} %get-tuple-element.22.a_hbm, bf16[4,512,768]{2,1,0:T(8,128)(2,1)} %get-tuple-element.23.df_hbm, bf16[4,4,512,768]{3,2,1,0:T(8,128)(2,1)} %get-tuple-element.24.h_hbm, ...), custom_call_target="tpu_custom_call" | custom-call | tf_op jit(solution)/shard_map/pallas_call | solution.py:826
  252.4 0.8 slice_bitcast_fusion
  253.2 1.6 fusion
  254.8 0.6 copy.24
  255.4 0.0 copy-start
  255.4 6.7 %copy.29 = f32[1,4,512,768]{3,2,1,0:T(8,128)} copy(f32[1,4,512,768]{3,2,1,0:T(8,128)} %get-tuple-element.45) | data formatting | bytes 12582912
  262.2 0.0 slice-start
  262.2 0.0 slice-start.1
  262.2 6.5 %copy.30 = f32[1,4,512,768]{3,2,1,0:T(8,128)} copy(f32[1,4,512,768]{3,2,1,0:T(8,128)} %get-tuple-element.46) | data formatting | bytes 12582912
  268.6 0.0 copy-done
  268.6 0.0 slice-start.2
  268.6 3.7 %copy.31 = f32[1,768,3072]{2,1,0:T(8,128)} copy(f32[1,768,3072]{2,1,0:T(8,128)S(1)} %copy-done) | data formatting | bytes 18874368
  272.4 0.0 slice-done
  272.4 0.0 slice-done.1
  272.4 0.0 slice-done.2
  272.4 3.7 %copy.32 = f32[1,3072,768]{2,1,0:T(8,128)} copy(f32[1,3072,768]{2,1,0:T(8,128)S(1)} %bitcast.6) | data formatting | bytes 18874368
  (2 shorter events, 0.0 us)
Async XLA Ops:
  255.4 13.2 %copy-start = (f32[1,768,3072]{2,1,0:T(8,128)S(1)}, f32[1,768,3072]{2,1,0:T(8,128)}, u32[]{:S(2)}) copy-start(f32[1,768,3072]{2,1,0:T(8,128)} %get-tuple-element.49) | copy-start | bytes 28311556
  262.2 10.2 %slice-start = ((s8[9437184]{0:T(1024)(128)(4,1)}), s8[4194304]{0:T(1024)(128)(4,1)S(1)}, s32[]{:S(2)}) async-start(s8[9437184]{0:T(1024)(128)(4,1)} %bitcast.5), calls=%async_computation | async-start | bytes 8388608
  262.2 10.2 %slice-start.1 = ((s8[9437184]{0:T(1024)(128)(4,1)}), s8[4194304]{0:T(1024)(128)(4,1)S(1)}, s32[]{:S(2)}) async-start(s8[9437184]{0:T(1024)(128)(4,1)} %bitcast.5), calls=%async_computation.1 | async-start | bytes 8388608
  268.6 3.8 %slice-start.2 = ((s8[9437184]{0:T(1024)(128)(4,1)}), s8[1048576]{0:T(1024)(128)(4,1)S(1)}, s32[]{:S(2)}) async-start(s8[9437184]{0:T(1024)(128)(4,1)} %bitcast.5), calls=%async_computation.2 | async-start | bytes 2097152

commit v4 on v3

--- a/solution.py
+++ b/solution.py
@@ -57,7 +57,7 @@
 
 def layers_kernel(
     count, rows, width, blocks, fb,
-    bucket, plan, norm_ref, upb_ref, in_hbm, cot_hbm, wu_hbm, wd_hbm, htab_hbm, stab_hbm,
+    bucket, plan, g1_ref, b1_ref, g2_ref, b2_ref, bd_ref, upb_ref, in_hbm, cot_hbm, wu_hbm, wd_hbm, htab_hbm, stab_hbm,
     act_hbm, grad_hbm, h_hbm, du_hbm, a_hbm, df_hbm, small_ref,
     wu, wd, htab, stab, inbuf, recv, sendbuf, deriv, xh1, xh2, rstd,
     hst, pq, u0, u1, acc, alow, dlow, yst, xst, sums,
@@ -78,18 +78,21 @@
     htab_copy = pltpu.make_async_copy(htab_hbm, htab, t_sem.at[1])
     stab_copy = pltpu.make_async_copy(stab_hbm, stab, t_sem.at[2])
 
+    def start_weights():
+        for b in range(blocks):
+            wu_copy(b).start()
+            wd_copy(b).start()
+
     @pl.when(first)
     def _():
         in_copy.start()
 
     htab_copy.start()
     stab_copy.start()
-    for b in range(blocks):
-        wu_copy(b).start()
-        wd_copy(b).start()
 
     @pl.when(jnp.logical_not(first))
     def _():
+        start_weights()
         cot_copy.start()
 
     sums[...] = jnp.zeros_like(sums)
@@ -142,11 +145,7 @@
     tiles = [[slice(r, r + span) for r in range(h.start, h.stop, span)] for h in halves]
     order = [(i, b) for i in range(2) for b in range(blocks)]
     buffers = (u0, u1)
-    g1 = norm_ref[0:1, :]
-    b1 = norm_ref[1:2, :]
-    g2 = norm_ref[2:3, :]
-    b2 = norm_ref[3:4, :]
-    bd = norm_ref[4:5, :]
+    g1, b1, g2, b2, bd = (ref[...] for ref in (g1_ref, b1_ref, g2_ref, b2_ref, bd_ref))
 
     def normalized(values):
         centered = values - jnp.mean(values, axis=-1, keepdims=True)
@@ -187,6 +186,7 @@
         @pl.when(jnp.logical_and(step == 0, first))
         def _():
             in_copy.wait()
+            start_weights()
 
         @pl.when(first)
         def _():
@@ -258,8 +258,9 @@
                 xh2[k, part, :] = unit.astype(BF)
                 rstd[k, part, 1:2] = scale
                 value = unit * g2 + b2
-                yst[part, :] = value
-                sendbuf[k, part, :] = value.astype(BF)
+                rounded = value.astype(BF)
+                yst[part, :] = rounded
+                sendbuf[k, part, :] = rounded
 
             @pl.when(first)
             def _():
@@ -339,7 +340,7 @@
         for i, part in enumerate(halves):
             value = acc[part, :] + dot(pq[0, part, :], htab[0]) + dot(pq[1, part, :], htab[1])
             rounded = value.astype(BF)
-            xst[part, :] = jnp.where(first, value, rounded.astype(F32))
+            xst[part, :] = rounded
             sendbuf[k, part, :] = rounded
 
             @pl.when(jnp.logical_not(first))
@@ -400,15 +401,15 @@
     return pl.pallas_call(
         body,
         out_shape=(
-            shape((1, count, rows, width), F32),
-            shape((1, count, rows, width), F32),
+            shape((1, count, rows, width), BF),
+            shape((1, count, rows, width), BF),
             shape((blocks, count, rows, fb), BF),
             shape((blocks, count, rows, fb), BF),
             shape((count, rows, width), BF),
             shape((count, rows, width), BF),
             shape((16, width), F32),
         ),
-        in_specs=[smem, smem, vmem, vmem] + [any_spec] * 6,
+        in_specs=[smem, smem] + [vmem] * 6 + [any_spec] * 6,
         out_specs=(any_spec,) * 6 + (vmem,),
         scratch_shapes=[
             pltpu.VMEM((blocks, width, fb), BF),
@@ -429,8 +430,8 @@
             pltpu.VMEM((rows, width), F32),
             pltpu.VMEM((rows, width), BF),
             pltpu.VMEM((rows, width), BF),
-            pltpu.VMEM((rows, width), F32),
-            pltpu.VMEM((rows, width), F32),
+            pltpu.VMEM((rows, width), BF),
+            pltpu.VMEM((rows, width), BF),
             pltpu.VMEM((5 + blocks, 8, width), F32),
             pltpu.SemaphoreType.DMA((2 * blocks,)),
             pltpu.SemaphoreType.DMA((3,)),
@@ -443,7 +444,7 @@
             collective_id=0, has_side_effects=True, vmem_limit_bytes=63 * 2**20
         ),
         cost_estimate=pl.CostEstimate(flops=flops, bytes_accessed=60 * 2**20, transcendentals=0),
-    )(bucket, plan, norms, up_bias, inputs, cotangent, up_weight, down_weight, htab, stab)
+    )(bucket, plan, *norms, up_bias, inputs, cotangent, up_weight, down_weight, htab, stab)
 
 
 KINDS = 13
@@ -515,20 +516,12 @@
     @pl.when(has_out)
     def _():
         pl.semaphore_signal(barrier, inc=1, device_id={"dp": outward}, device_id_type=pl.DeviceIdType.MESH)
-        pl.semaphore_wait(barrier, steps + 2)
-
-    @pl.when(edge)
-    def _():
-        pl.semaphore_wait(barrier, steps + 1)
 
     def small_copy(s):
         return pltpu.make_async_remote_copy(
             src_ref=sm.at[s], dst_ref=smin.at[s], send_sem=sm_send.at[s], recv_sem=sm_recv.at[s],
             device_id={"dp": partner(s)}, device_id_type=pl.DeviceIdType.MESH,
         )
-
-    sm[0] = small_ref[...]
-    small_copy(0).start()
 
     def message(kind, u, src, dst, target):
         return pltpu.make_async_remote_copy(
@@ -599,28 +592,8 @@
     def plus(left, right):
         return (left.astype(F32) + right.astype(F32)).astype(BF)
 
-    def compute(u):
+    def product(u):
         slot = u % RING
-        x_wait(u)
-
-        @pl.when(u + 2 < units)
-        def _():
-            x_start(u + 2)
-
-        @pl.when(u >= RING)
-        def _():
-            c1(u - RING).wait_send()
-
-        @pl.when(u == 0)
-        def _():
-            df_copy.wait()
-
-        @pl.when(u == half)
-        def _():
-            a_copy.wait()
-            for k in range(count):
-                at[:, k * rows : (k + 1) * rows] = abuf[k].T
-
         block = xb.at[u % 3]
 
         @pl.when(u < half)
@@ -637,6 +610,28 @@
             value = dot(at[...], block[...].reshape(count * rows, wide))
             prod[slot] = value.astype(BF).reshape(8, width // 8, wide)
 
+    def compute(u):
+        x_wait(u)
+
+        @pl.when(u + 2 < units)
+        def _():
+            x_start(u + 2)
+
+        @pl.when(u >= RING)
+        def _():
+            c1(u - RING).wait_send()
+
+        @pl.when(u == 1)
+        def _():
+            a_copy.wait()
+
+        for k in range(count):
+
+            @pl.when(u == 2 * k + 2)
+            def _():
+                at[:, k * rows : (k + 1) * rows] = abuf[k].T
+
+        product(u)
         c1(u).start()
 
     def stage1(u):
@@ -740,7 +735,7 @@
             for t in range(width // wide):
                 up_copy(half, t, u % 2).wait()
 
-        stage[u % 2] = res[u].reshape(width, wide).astype(F32)
+        stage[u % 2] = res[u].reshape(width, wide)
 
         @pl.when(u < half)
         def _():
@@ -755,7 +750,7 @@
     stages = (stage1, stage2, stage3, stage4, stage5, stage6, stage7)
 
     def one(i, carry):
-        @pl.when(i < units)
+        @pl.when(jnp.logical_and(i > 0, i < units))
         def _():
             compute(i)
 
@@ -777,6 +772,22 @@
 
         return carry
 
+    df_copy.wait()
+    x_wait(0)
+    x_start(2)
+    product(0)
+    sm[0] = small_ref[...]
+
+    @pl.when(has_out)
+    def _():
+        pl.semaphore_wait(barrier, steps + 2)
+
+    @pl.when(edge)
+    def _():
+        pl.semaphore_wait(barrier, steps + 1)
+
+    c1(0).start()
+    small_copy(0).start()
     lax.fori_loop(0, units + LAGS[-1], one, 0)
 
     small_out[...] = sm[steps]
@@ -825,7 +836,7 @@
     body = functools.partial(grads_kernel, dp, count, rows, width, units, wide, 3)
     return pl.pallas_call(
         body,
-        out_shape=(shape((1, hidden, width), F32), shape((1, width, hidden), F32), shape(small.shape, F32)),
+        out_shape=(shape((1, hidden, width), BF), shape((1, width, hidden), BF), shape(small.shape, F32)),
         in_specs=[any_spec] * 4 + [vmem],
         out_specs=(any_spec, any_spec, vmem),
         scratch_shapes=[
@@ -836,7 +847,7 @@
             pltpu.VMEM((RING, 8, piece, wide), BF),
             pltpu.VMEM((units, 4, piece, wide), BF),
             pltpu.VMEM((units, 8, piece, wide), BF),
-            pltpu.VMEM((2, width, wide), F32),
+            pltpu.VMEM((2, width, wide), BF),
             pltpu.VMEM((units, 4, piece, wide), BF),
             pltpu.VMEM((units, piece, wide), BF),
             pltpu.VMEM((units, piece, wide), BF),
@@ -860,24 +871,62 @@
     )(a, df, h, du, small)
 
 
+def widen_kernel(act, grad, down, up, small, act_out, grad_out, g1, b1, up_out, upb, down_out, bd, g2, b2):
+    act_out[...] = act[...].astype(F32)
+    grad_out[...] = grad[...].astype(F32)
+    up_out[...] = up[...].astype(F32)
+    down_out[...] = down[...].astype(F32)
+
+    @pl.when(pl.program_id(0) == 0)
+    def _():
+        width = small.shape[-1]
+        for n, out in enumerate((g1, b1, g2, b2, bd)):
+            out[...] = small[n : n + 1, :]
+        for b in range(upb.shape[-1] // width):
+            upb[:, b * width : (b + 1) * width] = small[5 + b : 6 + b, :]
+
+
+def run_widen(act, grad, down, up, small):
+    count, rows, width = act.shape[1:]
+    hidden = down.shape[1]
+    grid = 4 * count
+    token = pl.BlockSpec((1, 1, rows // 4, width), lambda i: (0, i // 4, i % 4, 0))
+    tall = pl.BlockSpec((1, hidden // grid, width), lambda i: (0, i, 0))
+    flat = pl.BlockSpec((1, width // grid, hidden), lambda i: (0, i, 0))
+
+    def whole(*extent):
+        return pl.BlockSpec(extent, lambda i: (0, 0))
+
+    shape = jax.ShapeDtypeStruct
+    row = shape((1, width), F32)
+    line = whole(1, width)
+    return pl.pallas_call(
+        widen_kernel,
+        grid=(grid,),
+        in_specs=[token, token, tall, flat, whole(*small.shape)],
+        out_specs=(token, token, line, line, flat, whole(1, hidden), tall, line, line, line),
+        out_shape=(
+            shape(act.shape, F32), shape(grad.shape, F32), row, row, shape(up.shape, F32),
+            shape((1, hidden), F32), shape(down.shape, F32), row, row, row,
+        ),
+        compiler_params=pltpu.CompilerParams(
+            dimension_semantics=("arbitrary",), vmem_limit_bytes=60 * 2**20
+        ),
+    )(act, grad, down, up, small)
+
+
 def per_device(
     inputs, bucket, plan, cotangent, norm1_gain, norm1_bias, up_weight, up_bias,
     down_weight, down_bias, norm2_gain, norm2_bias,
 ):
     count, rows, width = inputs.shape
     hidden = up_weight.shape[-1]
-    norms = jnp.concatenate(
-        [norm1_gain, norm1_bias, norm2_gain, norm2_bias, down_bias, jnp.zeros((3, width), F32)]
-    )
+    norms = (norm1_gain, norm1_bias, norm2_gain, norm2_bias, down_bias)
     activations, input_grad, h, du, a, df, small = run_layers(
         bucket, plan, norms, up_bias.reshape(-1, 1, width), inputs, cotangent, up_weight, down_weight
     )
     down_grad, up_grad, small = run_grads(lax.axis_size("dp"), a, df, h, du, small)
-    blocks = hidden // width
-    return (
-        activations, input_grad, small[0:1], small[1:2], up_grad,
-        small[5 : 5 + blocks].reshape(1, hidden), down_grad, small[4:5], small[2:3], small[3:4],
-    )
+    return run_widen(activations, input_grad, down_grad, up_grad, small)
 
 
 def solution(mesh):

time: 277 us -> 269 us (0.971)
  local copies, waits for them, and re-layouts: 25.1 us -> 0 us
  Pallas kernels: 250 us -> 267 us
    unnamed x14 -> x0, local copies, waits for them, and re-layouts: 22.1 us -> none
    pallas_call x2 -> x3, Pallas kernels: 250 us -> 267 us  [the longest x1 137 us: run_layers(): pl.pallas_call(body, out_shape=(shape((1, count, rows, width), BF), shape...]
where the time goes in v4:
time: 269 us; the launch traced here: 268 us
  Pallas kernels  267 us (99%)
    pallas_call x1, Pallas kernels, run_layers(): pl.pallas_call(body, out_shape=(shape((1, count, rows, width), BF), shape...  137 us
    pallas_call x1, Pallas kernels, run_grads(): pl.pallas_call(body, out_shape=(shape((1, hidden, width), BF), shape((1,...  111 us
    pallas_call x1, Pallas kernels, run_widen(): pl.pallas_call(widen_kernel, grid=(grid,), in_specs=[token, token, tall,...  18.9 us

profile of v4, /device:TPU:0, one launch (start us, length us, event | category | flops | bytes accessed | tf_op | source)
XLA Modules:
  0.0 267.7 jit_solution(6928590434017301532)
XLA Ops:
  0.6 137.1 %shard_map.213 = (bf16[1,4,512,768]{3,2,1,0:T(8,128)(2,1)}, bf16[1,4,512,768]{3,2,1,0:T(8,128)(2,1)}, bf16[4,4,512,768]{3,2,1,0:T(8,128)(2,1)}, bf16[4,4,512,768...) custom-call(s32[4]{0:T(128)} %bucket.1, s32[4]{0:T(128)} %plan.1, ...), custom_call_target="tpu_custom_call" | custom-call | flops 74088185856 | bytes 62914560 | tf_op jit(solution)/shard_map/pallas_call | solution.py:401
  137.7 110.8 %shard_map.214 = (bf16[1,3072,768]{2,1,0:T(8,128)(2,1)}, bf16[1,768,3072]{2,1,0:T(8,128)(2,1)}, f32[16,768]{1,0:T(8,128)}) custom-call(bf16[4,512,768]{2,1,0:T(8,128)(2,1)} %get-tuple-element.22.a_hbm, bf16[4,512,768]{2,1,0:T(8,128)(2,1)} %get-tuple-element.23.df_hbm, bf16[4,4,512,768]{3,2,1,0:T(8,128)(2,1)} %get-tuple-element.24.h_hbm, ...), custom_call_target="tpu_custom_call" | custom-call | tf_op jit(solution)/shard_map/pallas_call | solution.py:837
  248.6 18.9 %shard_map.215 = (f32[1,4,512,768]{3,2,1,0:T(8,128)}, f32[1,4,512,768]{3,2,1,0:T(8,128)}, f32[1,768]{1,0:T(1,128)}, f32[1,768]{1,0:T(1,128)}, f32[1,768,3072]{2,...) custom-call(bf16[1,4,512,768]{3,2,1,0:T(8,128)(2,1)} %get-tuple-elem, ...), custom_call_target="tpu_custom_call" | custom-call | tf_op jit(solution)/shard_map/pallas_call | solution.py:903

commit v5 on v4

--- a/solution.py
+++ b/solution.py
@@ -61,10 +61,12 @@
     act_hbm, grad_hbm, h_hbm, du_hbm, a_hbm, df_hbm, small_ref,
     wu, wd, htab, stab, inbuf, recv, sendbuf, deriv, xh1, xh2, rstd,
     hst, pq, u0, u1, acc, alow, dlow, yst, xst, sums,
-    w_sem, t_sem, o_sem, h_sem, send_sem, recv_sem,
+    w_sem, t_sem, o_sem, h_sem, send_sem, recv_sem, turn_sem,
 ):
     first = lax.axis_index("pipe") == 0
     partner = 1 - lax.axis_index("pipe")
+    core = lax.axis_index("dp") % 2
+    sibling = lax.axis_index("dp") + 1 - 2 * core
     last = blocks - 1
 
     def wu_copy(b):
@@ -99,7 +101,8 @@
 
     barrier = pltpu.get_barrier_semaphore()
     pl.semaphore_signal(barrier, inc=1, device_id={"pipe": partner}, device_id_type=pl.DeviceIdType.MESH)
-    pl.semaphore_wait(barrier, 1)
+    pl.semaphore_signal(barrier, inc=1, device_id={"dp": sibling}, device_id_type=pl.DeviceIdType.MESH)
+    pl.semaphore_wait(barrier, 2)
 
     span = rows // CHUNKS
 
@@ -262,9 +265,25 @@
                 yst[part, :] = rounded
                 sendbuf[k, part, :] = rounded
 
+            if i == 0:
+
+                @pl.when(jnp.logical_and(first, core + k > 0))
+                def _():
+                    pl.semaphore_wait(turn_sem, 1)
+
             @pl.when(first)
             def _():
                 leave(k, i)
+
+            if i == 1:
+
+                @pl.when(jnp.logical_and(first, k + core < count))
+                def _():
+                    for c in range(CHUNKS):
+                        chunk_copy(k, c).wait_send()
+                    pl.semaphore_signal(
+                        turn_sem, inc=1, device_id={"dp": sibling}, device_id_type=pl.DeviceIdType.MESH
+                    )
 
         pipelined(up, activate, down, before, after)
         for b in range(blocks):
@@ -279,7 +298,7 @@
         def _():
             cot_copy.wait()
 
-        @pl.when(first)
+        @pl.when(jnp.logical_and(first, k + core == count))
         def _():
             for c in range(CHUNKS):
                 chunk_copy(k, c).wait_send()
@@ -439,6 +458,7 @@
             pltpu.SemaphoreType.DMA((blocks,)),
             pltpu.SemaphoreType.DMA((count, CHUNKS)),
             pltpu.SemaphoreType.DMA((count, CHUNKS)),
+            pltpu.SemaphoreType.REGULAR,
         ],
         compiler_params=pltpu.CompilerParams(
             collective_id=0, has_side_effects=True, vmem_limit_bytes=63 * 2**20

time: 269 us -> 262 us (0.974)
  Pallas kernels: 267 us -> 260 us
    pallas_call x1, Pallas kernels: 137 us -> 121 us  [run_layers(): pl.pallas_call(body, out_shape=(shape((1, count, rows, width), BF), shape...]
    pallas_call x1, Pallas kernels: 111 us -> 120 us  [run_grads(): pl.pallas_call(body, out_shape=(shape((1, hidden, width), BF), shape((1,...]
where the time goes in v5:
time: 262 us; the launch traced here: 261 us
  Pallas kernels  260 us (99%)
    pallas_call x1, Pallas kernels, run_layers(): pl.pallas_call(body, out_shape=(shape((1, count, rows, width), BF), shape...  121 us
    pallas_call x1, Pallas kernels, run_grads(): pl.pallas_call(body, out_shape=(shape((1, hidden, width), BF), shape((1,...  120 us
    pallas_call x1, Pallas kernels, run_widen(): pl.pallas_call(widen_kernel, grid=(grid,), in_specs=[token, token, tall,...  18.9 us

profile of v5, /device:TPU:0, one launch (start us, length us, event | category | flops | bytes accessed | tf_op | source)
XLA Modules:
  0.0 261.1 jit_solution(960810217724479465)
XLA Ops:
  0.6 121.4 %shard_map.213 = (bf16[1,4,512,768]{3,2,1,0:T(8,128)(2,1)}, bf16[1,4,512,768]{3,2,1,0:T(8,128)(2,1)}, bf16[4,4,512,768]{3,2,1,0:T(8,128)(2,1)}, bf16[4,4,512,768...) custom-call(s32[4]{0:T(128)} %bucket.1, s32[4]{0:T(128)} %plan.1, ...), custom_call_target="tpu_custom_call" | custom-call | flops 74088185856 | bytes 62914560 | tf_op jit(solution)/shard_map/pallas_call | solution.py:420
  122.1 120.0 %shard_map.214 = (bf16[1,3072,768]{2,1,0:T(8,128)(2,1)}, bf16[1,768,3072]{2,1,0:T(8,128)(2,1)}, f32[16,768]{1,0:T(8,128)}) custom-call(bf16[4,512,768]{2,1,0:T(8,128)(2,1)} %get-tuple-element.22.a_hbm, bf16[4,512,768]{2,1,0:T(8,128)(2,1)} %get-tuple-element.23.df_hbm, bf16[4,4,512,768]{3,2,1,0:T(8,128)(2,1)} %get-tuple-element.24.h_hbm, ...), custom_call_target="tpu_custom_call" | custom-call | tf_op jit(solution)/shard_map/pallas_call | solution.py:857
  242.1 18.9 %shard_map.215 = (f32[1,4,512,768]{3,2,1,0:T(8,128)}, f32[1,4,512,768]{3,2,1,0:T(8,128)}, f32[1,768]{1,0:T(1,128)}, f32[1,768]{1,0:T(1,128)}, f32[1,768,3072]{2,...) custom-call(bf16[1,4,512,768]{3,2,1,0:T(8,128)(2,1)} %get-tuple-elem, ...), custom_call_target="tpu_custom_call" | custom-call | tf_op jit(solution)/shard_map/pallas_call | solution.py:923

commit v6 on v5

--- a/solution.py
+++ b/solution.py
@@ -177,19 +177,18 @@
         down(*order[-1])
         after(1)
 
-    def forward(k, step):
+    def forward(k, opening):
         source = plan[k]
         length = bucket[k]
         level = jnp.where(length == rows, 2, jnp.where(length * 2 == rows, 1, 0))
 
-        @pl.when(step == 0)
-        def _():
+        if opening:
             htab_copy.wait()
 
-        @pl.when(jnp.logical_and(step == 0, first))
-        def _():
-            in_copy.wait()
-            start_weights()
+            @pl.when(first)
+            def _():
+                in_copy.wait()
+                start_weights()
 
         @pl.when(first)
         def _():
@@ -204,18 +203,13 @@
             pq[0, part] = dot(recv[k, part], htab[0]).astype(BF)
             pq[1, part] = dot(recv[k, part], htab[1]).astype(BF)
 
-        @pl.when(step == 0)
-        def _():
+        if opening:
             stab_copy.wait()
-
-        @pl.when(step > 0)
-        def _():
+        else:
             for b in range(blocks):
                 h_copy(k, b).wait()
-
-        @pl.when(k > 0)
-        def _():
             a_copy(k).wait()
+            act_copy(k).wait()
 
         for part in halves:
             mixed = dot(stab[level, 0, part, :], pq[0]) + dot(stab[level, 1, part, :], pq[1])
@@ -225,17 +219,10 @@
             value = unit * g1 + b1
             alow[part, :] = value.astype(BF)
             acc[part, :] = value + bd
-        a_copy(k).start()
-
-        @pl.when(step == 0)
-        def _():
+        if opening:
             for b in range(blocks):
                 wu_copy(b).wait()
                 wd_copy(b).wait()
-
-        @pl.when(k > 0)
-        def _():
-            act_copy(k).wait()
 
         def up(i, b, u):
             u[...] = dot(alow[halves[i], :], wu[b])
@@ -248,6 +235,8 @@
             slope = level_half + value * (1.0 - level_half) * (2.0 * TANH_IN + 6.0 * TANH_CUBE * square)
             hst[b, halves[i], :] = value.astype(BF)
             deriv[k, b, halves[i], :] = slope.astype(BF)
+            if i == 1:
+                h_copy(k, b).start()
 
         def down(i, b):
             acc[halves[i], :] += dot(hst[b, halves[i], :], wd[b])
@@ -286,11 +275,10 @@
                     )
 
         pipelined(up, activate, down, before, after)
-        for b in range(blocks):
-            h_copy(k, b).start()
+        a_copy(k).start()
         act_copy(k).start()
 
-    def backward(k, step):
+    def backward(k):
         length = bucket[k]
         level = jnp.where(length == rows, 2, jnp.where(length * 2 == rows, 1, 0))
 
@@ -307,6 +295,9 @@
         def _():
             df_copy(k).wait()
             grad_copy(k).wait()
+
+        for b in range(blocks):
+            du_copy(k, b).wait()
 
         def before(i):
             @pl.when(first)
@@ -323,9 +314,6 @@
                 sums[2] += fold8(grad * unit)
                 sums[3] += fold8(grad)
                 sums[4] += fold8(rounded.astype(F32))
-            if i == 0:
-                for b in range(blocks):
-                    du_copy(k, b).wait()
 
         def up(i, b, u):
             u[...] = dot_t(dlow[halves[i], :], wd[b])
@@ -334,6 +322,8 @@
             rounded = (u[...] * deriv[k, b, halves[i], :].astype(F32)).astype(BF)
             hst[b, halves[i], :] = rounded
             sums[5 + b] += fold8(rounded.astype(F32))
+            if i == 1:
+                du_copy(k, b).start()
 
         def down(i, b):
             acc[halves[i], :] += dot_t(hst[b, halves[i], :], wu[b])
@@ -349,10 +339,6 @@
                 sums[1] += fold8(grad)
 
         pipelined(up, activate, down, before, after)
-        df_copy(k).start()
-        for b in range(blocks):
-            du_copy(k, b).start()
-
         pq[0] = dot(stab[level, 0], recv[k]).astype(BF)
         pq[1] = dot(stab[level, 1], recv[k]).astype(BF)
 
@@ -366,6 +352,7 @@
             def _():
                 leave(k, i)
 
+        df_copy(k).start()
         grad_copy(k).start()
 
     def one(step, carry):
@@ -374,15 +361,16 @@
 
         @pl.when(forwards)
         def _():
-            forward(k, step)
+            forward(k, False)
 
         @pl.when(jnp.logical_not(forwards))
         def _():
-            backward(k, step)
+            backward(k)
 
         return carry
 
-    lax.fori_loop(0, 2 * count, one, 0)
+    forward(0, True)
+    lax.fori_loop(1, 2 * count, one, 0)
 
     end = count - 1
 

time: 262 us -> 258 us (0.985)
  Pallas kernels: 260 us -> 257 us
where the time goes in v6:
time: 258 us
  Pallas kernels  257 us (100%)
    pallas_call x1, Pallas kernels, run_layers(): pl.pallas_call(body, out_shape=(shape((1, count, rows, width), BF), shape...  120 us
    pallas_call x1, Pallas kernels, run_grads(): pl.pallas_call(body, out_shape=(shape((1, hidden, width), BF), shape((1,...  118 us
    pallas_call x1, Pallas kernels, run_widen(): pl.pallas_call(widen_kernel, grid=(grid,), in_specs=[token, token, tall,...  18.9 us

profile of v6, /device:TPU:0, one launch (start us, length us, event | category | flops | bytes accessed | tf_op | source)
XLA Modules:
  0.0 257.8 jit_solution(8717662128822428960)
XLA Ops:
  0.6 120.5 %shard_map.213 = (bf16[1,4,512,768]{3,2,1,0:T(8,128)(2,1)}, bf16[1,4,512,768]{3,2,1,0:T(8,128)(2,1)}, bf16[4,4,512,768]{3,2,1,0:T(8,128)(2,1)}, bf16[4,4,512,768...) custom-call(s32[4]{0:T(128)} %bucket.1, s32[4]{0:T(128)} %plan.1, ...), custom_call_target="tpu_custom_call" | custom-call | flops 74088185856 | bytes 62914560 | tf_op jit(solution)/shard_map/pallas_call | solution.py:408
  121.1 117.6 %shard_map.214 = (bf16[1,3072,768]{2,1,0:T(8,128)(2,1)}, bf16[1,768,3072]{2,1,0:T(8,128)(2,1)}, f32[16,768]{1,0:T(8,128)}) custom-call(bf16[4,512,768]{2,1,0:T(8,128)(2,1)} %get-tuple-element.22.a_hbm, bf16[4,512,768]{2,1,0:T(8,128)(2,1)} %get-tuple-element.23.df_hbm, bf16[4,4,512,768]{3,2,1,0:T(8,128)(2,1)} %get-tuple-element.24.h_hbm, ...), custom_call_target="tpu_custom_call" | custom-call | tf_op jit(solution)/shard_map/pallas_call | solution.py:845
  238.7 18.9 %shard_map.215 = (f32[1,4,512,768]{3,2,1,0:T(8,128)}, f32[1,4,512,768]{3,2,1,0:T(8,128)}, f32[1,768]{1,0:T(1,128)}, f32[1,768]{1,0:T(1,128)}, f32[1,768,3072]{2,...) custom-call(bf16[1,4,512,768]{3,2,1,0:T(8,128)(2,1)} %get-tuple-elem, ...), custom_call_target="tpu_custom_call" | custom-call | tf_op jit(solution)/shard_map/pallas_call | solution.py:911

commit v7 on v6

--- a/solution.py
+++ b/solution.py
@@ -874,7 +874,7 @@
             pltpu.SemaphoreType.DMA((steps,)),
         ],
         compiler_params=pltpu.CompilerParams(
-            collective_id=1, has_side_effects=True, vmem_limit_bytes=60 * 2**20
+            collective_id=1, has_side_effects=True, vmem_limit_bytes=52 * 2**20
         ),
     )(a, df, h, du, small)
 
@@ -918,7 +918,7 @@
             shape((1, hidden), F32), shape(down.shape, F32), row, row, row,
         ),
         compiler_params=pltpu.CompilerParams(
-            dimension_semantics=("arbitrary",), vmem_limit_bytes=60 * 2**20
+            dimension_semantics=("arbitrary",), vmem_limit_bytes=12 * 2**20
         ),
     )(act, grad, down, up, small)
 

time: 258 us -> 255 us (0.988)
  Pallas kernels: 257 us -> 248 us
  local copies, waits for them, and re-layouts: 0 us -> 5.47 us
    pallas_call x1, Pallas kernels: 18.9 us -> 11.5 us  [run_widen(): pl.pallas_call(widen_kernel, grid=(grid,), in_specs=[token, token, tall,...]
    unnamed x0 -> x10, local copies, waits for them, and re-layouts: none -> 5.47 us
where the time goes in v7:
time: 255 us
  Pallas kernels  248 us (97%)
  local copies, waits for them, and re-layouts  5.47 us (2%)
    pallas_call x1, Pallas kernels, run_layers(): pl.pallas_call(body, out_shape=(shape((1, count, rows, width), BF), shape...  120 us
    pallas_call x1, Pallas kernels, run_grads(): pl.pallas_call(body, out_shape=(shape((1, hidden, width), BF), shape((1,...  116 us
    pallas_call x1, Pallas kernels, run_widen(): pl.pallas_call(widen_kernel, grid=(grid,), in_specs=[token, token, tall,...  11.5 us
    unnamed x10, local copies, waits for them, and re-layouts  5.47 us

profile of v7, /device:TPU:0, one launch (start us, length us, event | category | flops | bytes accessed | tf_op | source)
XLA Modules:
  0.0 254.7 jit_solution(16074803303908901220)
XLA Ops:
  0.6 120.4 %shard_map.213 = (bf16[1,4,512,768]{3,2,1,0:T(8,128)(2,1)}, bf16[1,4,512,768]{3,2,1,0:T(8,128)(2,1)}, bf16[4,4,512,768]{3,2,1,0:T(8,128)(2,1)}, bf16[4,4,512,768...) custom-call(s32[4]{0:T(128)} %bucket.1, s32[4]{0:T(128)} %plan.1, ...), custom_call_target="tpu_custom_call" | custom-call | flops 74088185856 | bytes 62914560 | tf_op jit(solution)/shard_map/pallas_call | solution.py:408
  121.0 0.0 copy-start.4
  121.0 0.8 copy-done.4
  121.8 0.0 copy-start.2
  121.8 0.0 copy-start.3
  121.8 116.4 %shard_map.214 = (bf16[1,3072,768]{2,1,0:T(8,128)(2,1)}, bf16[1,768,3072]{2,1,0:T(8,128)(2,1)}, f32[16,768]{1,0:T(8,128)S(1)}) custom-call(bf16[4,512,768]{2,1,0:T(8,128)(2,1)} %get-tuple-element.22.a_hbm, bf16[4,512,768]{2,1,0:T(8,128)(2,1)} %get-tuple-element.23.df_hbm, bf16[4,4,512,768]{3,2,1,0:T(8,128)(2,1)} %get-tuple-element.24.h_hbm, ...), custom_call_target="tpu_custom_call" | custom-call | tf_op jit(solution)/shard_map/pallas_call | solution.py:845
  238.3 0.0 copy-done.2
  238.3 0.0 copy-done.3
  238.3 0.0 copy-start
  238.3 2.3 copy-done
  240.6 0.0 copy-start.1
  240.6 2.3 copy-done.1
  243.0 11.5 %shard_map.215 = (f32[1,4,512,768]{3,2,1,0:T(8,128)}, f32[1,4,512,768]{3,2,1,0:T(8,128)}, f32[1,768]{1,0:T(1,128)}, f32[1,768]{1,0:T(1,128)}, f32[1,768,3072]{2,...) custom-call(bf16[1,4,512,768]{3,2,1,0:T(8,128)(2,1)S(1)} %copy-done., ...), custom_call_target="tpu_custom_call" | custom-call | tf_op jit(solution)/shard_map/pallas_call | solution.py:911
Async XLA Ops:
  121.0 0.8 copy-start.4
  121.8 116.5 %copy-start.2 = (bf16[1,4,512,768]{3,2,1,0:T(8,128)(2,1)S(1)}, bf16[1,4,512,768]{3,2,1,0:T(8,128)(2,1)}, u32[]{:S(2)}) copy-start(bf16[1,4,512,768]{3,2,1,0:T(8,128)(2,1)} %get-tuple-element.20.act) | copy-start | bytes 9437188
  121.8 116.5 %copy-start.3 = (bf16[1,4,512,768]{3,2,1,0:T(8,128)(2,1)S(1)}, bf16[1,4,512,768]{3,2,1,0:T(8,128)(2,1)}, u32[]{:S(2)}) copy-start(bf16[1,4,512,768]{3,2,1,0:T(8,128)(2,1)} %get-tuple-element.21.grad) | copy-start | bytes 9437188
  238.3 2.3 copy-start
  240.6 2.3 copy-start.1
